TPU v7x, 256 devices: a whole 4x4x8 slice. The times are simulated.
256 devices in a mesh: seq: 8 (over z_hi, core), chan: 32 (over y, x, z_lo).
Axes of the slice: x: 4, y: 4, z: 8 (z_hi: 4, z_lo: 2; z = z_hi * 2 + z_lo), core: 2. Of those that a mesh axis runs over, the one named last changes fastest.
Arguments:
- signal: bfloat16 [4096, 4096], P('seq', 'chan'), may hold values from -6 to 6
- gating: bfloat16 [4096, 4096], P('seq', 'chan'), may hold values from -6 to 6
- filter_taps: bfloat16 [4096, 4096], P('seq', 'chan'), may hold values from -0.25 to 0.25
- skip_bias: float32 [4096], P('chan'), may hold values from -1 to 1
- out_weight: bfloat16 [4096, 4096], P(None, 'chan'), may hold values from -0.09375 to 0.09375
- test_matrix: bfloat16 [4096, 256], P('chan'), may hold values from -0.09375 to 0.09375
Outputs:
- mixed: bfloat16 [4096, 4096], P('seq', 'chan')
- sketch_y: float32 [4096, 256], P('seq')
- sketch_z: float32 [4096, 256], P('chan')
All inputs are finite; a program needn't handle non-finite values.
Results may differ from a plain program's by a relative error of at most 0.015.
Values may be sent and summed in bfloat16 or wider, within the bound.
A program may use at most 64 MiB of HBM per device.

v0:
```python
import math

import jax
import jax.numpy as jnp
from jax import lax
from jax.sharding import PartitionSpec as P

precise = lax.Precision.HIGHEST


def angle_table(first, second, period, sign):
    product = first[:, None] * second[None, :] % period
    angles = product.astype(jnp.float32) * (sign * 2.0 * math.pi / period)
    return (jnp.cos(angles), jnp.sin(angles))


def per_device(signal, gating, filter_taps, skip_bias, out_weight, test_matrix):
    rows_dev, channels = signal.shape
    shards = lax.axis_size("seq")
    my_index = lax.axis_index("seq")
    sub_rows = rows_dev // shards
    fft_len = 2 * shards * rows_dev
    freq_coarse = jnp.arange(2 * shards, dtype=jnp.int32)
    pieces = (
        lax.all_to_all(signal[None], "seq", split_axis=1, concat_axis=0, tiled=True),
        lax.all_to_all(filter_taps[None], "seq", split_axis=1, concat_axis=0, tiled=True),
    )
    small_cos, small_sin = angle_table(
        freq_coarse, jnp.arange(shards, dtype=jnp.int32), 2 * shards, -1.0
    )
    local_cols = my_index * sub_rows + jnp.arange(sub_rows, dtype=jnp.int32)
    twid_cos, twid_sin = angle_table(freq_coarse, local_cols, fft_len, -1.0)
    twid_cos = twid_cos[:, :, None]
    twid_sin = twid_sin[:, :, None]
    parts_list = []
    for values in pieces:
        source = values.astype(jnp.float32)
        real_part = jnp.einsum("kq,qbc->kbc", small_cos, source, precision=precise)
        imag_part = jnp.einsum("kq,qbc->kbc", small_sin, source, precision=precise)
        parts_list.append(real_part * twid_cos - imag_part * twid_sin)
        parts_list.append(real_part * twid_sin + imag_part * twid_cos)
    stacked = jnp.stack(parts_list)
    columns = lax.all_to_all(stacked, "seq", split_axis=1, concat_axis=2, tiled=True)
    all_rows = jnp.arange(rows_dev, dtype=jnp.int32)
    big_cos, big_sin = angle_table(all_rows, all_rows, rows_dev, -1.0)
    cos_part = jnp.einsum("kb,sjbc->sjkc", big_cos, columns, precision=precise)
    sin_part = jnp.einsum("kb,sjbc->sjkc", big_sin, columns, precision=precise)
    sig_re = cos_part[0] - sin_part[1]
    sig_im = cos_part[1] + sin_part[0]
    fil_re = cos_part[2] - sin_part[3]
    fil_im = cos_part[3] + sin_part[2]
    prod_re = sig_re * fil_re - sig_im * fil_im
    prod_im = sig_re * fil_im + sig_im * fil_re
    back_re = jnp.einsum("kb,jkc->jbc", big_cos, prod_re, precision=precise) + jnp.einsum(
        "kb,jkc->jbc", big_sin, prod_im, precision=precise
    )
    back_im = jnp.einsum("kb,jkc->jbc", big_cos, prod_im, precision=precise) - jnp.einsum(
        "kb,jkc->jbc", big_sin, prod_re, precision=precise
    )
    my_freq = 2 * my_index + jnp.arange(2, dtype=jnp.int32)
    inv_cos, inv_sin = angle_table(my_freq, all_rows, fft_len, 1.0)
    inv_cos = inv_cos[:, :, None]
    inv_sin = inv_sin[:, :, None]
    turned_re = back_re * inv_cos - back_im * inv_sin
    turned_im = back_re * inv_sin + back_im * inv_cos
    gathered_freq = lax.all_to_all(
        jnp.stack([turned_re, turned_im]), "seq", split_axis=2, concat_axis=1, tiled=True
    )
    out_cos, out_sin = angle_table(
        jnp.arange(shards, dtype=jnp.int32), freq_coarse, 2 * shards, 1.0
    )
    by_class = jnp.einsum("qk,kbc->qbc", out_cos, gathered_freq[0], precision=precise) - jnp.einsum(
        "qk,kbc->qbc", out_sin, gathered_freq[1], precision=precise
    )
    convolved = lax.all_to_all(by_class / fft_len, "seq", split_axis=0, concat_axis=1, tiled=True)[
        0
    ]
    gated = (
        gating.astype(jnp.float32) * (convolved + skip_bias[None, :] * signal.astype(jnp.float32))
    ).astype(jnp.bfloat16)
    projected = jnp.dot(
        lax.all_gather(gated, "chan", axis=1, tiled=True),
        out_weight,
        preferred_element_type=jnp.float32,
    )
    partial_y = jnp.dot(projected, test_matrix.astype(jnp.float32), precision=precise)
    sketch_y = lax.psum(partial_y, "chan")
    mixed = projected.astype(jnp.bfloat16)
    total_rows = rows_dev * shards
    partial_z = jnp.einsum("tc,tr->cr", projected, sketch_y, precision=precise) / total_rows
    sketch_z = lax.psum(partial_z.astype(jnp.bfloat16), "seq").astype(jnp.float32)
    return (mixed, sketch_y, sketch_z)


def solution(mesh):
    placed = (
        P("seq", "chan"),
        P("seq", "chan"),
        P("seq", "chan"),
        P("chan"),
        P(None, "chan"),
        P("chan", None),
    )
    return jax.shard_map(
        per_device,
        mesh=mesh,
        in_specs=placed,
        out_specs=(P("seq", "chan"), P("seq", None), P("chan", None)),
        check_vma=False,
    )
```

profile of v0, /device:TPU:1, one launch (start us, length us, event | category | flops | bytes accessed | tf_op | source)
XLA Modules:
  0.0 751.0 jit_solution(8850229393054781713)
XLA Ops:
  8.9 1.4 reduce.1
  11.0 10.0 %all-to-all-start.1 = ((bf16[8,2,4096]{2,1,0:T(2,128)(2,1)}), bf16[8,2,4096]{2,1,0:T(2,128)(2,1)S(1)}, u32[]{:S(2)}, u32[]{:S(2)}) async-start(bf16[8,2,4096]{2,1,0:T(2,128)(2,1)} %reshape.151), calls=%async_computation.1 | async-start | bytes 262144 | tf_op jit(solution)/shard_map/all_to_all | solution.py:26
  22.1 1.4 reduce
  24.4 4.6 all-to-all-done.1
  29.0 4.8 all-to-all-start
  34.9 6.9 all-to-all-done
  43.3 2.0 copy.41
  45.3 5.1 all-to-all-start.2
  50.5 44.0 %all-to-all-done.2 = f32[4,16,64,128]{3,2,0,1:T(8,128)S(1)} async-done(((f32[4,16,64,128]{3,2,0,1:T(8,128)}), f32[4,16,64,128]{3,2,0,1:T(8,128)S(1)}, u32[]{:S(2)}, u32[]{:S(2)}) %all-to-all-start.2) | async-done | bytes 2097184 | tf_op jit(solution)/shard_map/all_to_all | solution.py:43
  94.8 11.0 %convolution_bitcast_fusion = f32[4,2,512,128]{2,3,1,0:T(8,128)S(1)} fusion(f32[4,2,512,128]{3,2,1,0:T(8,128)S(1)} %bitcast.111), kind=kOutput, calls=%fused_computation.1 | convolution fusion | flops 3224895488 | bytes 4194304 | tf_op jit(solution)/shard_map/kb,sjbc->sjkc/dot_general | solution.py:47
  105.8 10.9 %convolution_bitcast_fusion.1 = f32[4,2,512,128]{2,3,1,0:T(8,128)S(1)} fusion(f32[4,2,512,128]{3,2,1,0:T(8,128)S(1)} %bitcast.112), kind=kOutput, calls=%fused_computation.2 | convolution fusion | flops 3224895488 | bytes 4194304 | tf_op jit(solution)/shard_map/kb,sjbc->sjkc/dot_general | solution.py:46
  117.2 5.5 fusion.9
  122.8 5.3 fusion.11
  128.1 5.3 convolution_subtract_fusion
  133.5 5.4 subtract_bitcast_fusion
  139.7 35.3 %all_to_all.66 = f32[2,2,512,128]{3,1,0,2:T(2,128)S(1)} all-to-all(f32[2,2,512,128]{3,1,0,2:T(2,128)S(1)} %copy.46), channel_id=1, replica_groups=mesh['seq'=8,'chan'=32] {'seq'}, dimensions={2} | all-to-all | bytes 2097152 | tf_op jit(solution)/shard_map/all_to_all | solution.py:66
  177.0 17.1 %all_to_all.67 = f32[8,64,128]{2,1,0:T(8,128)S(1)} all-to-all(f32[8,64,128]{2,1,0:T(8,128)S(1)} %copy.50), channel_id=1, replica_groups=mesh['seq'=8,'chan'=32] {'seq'}, dimensions={0} | all-to-all | bytes 524288 | tf_op jit(solution)/shard_map/all_to_all | solution.py:75
  194.9 140.4 %all-gather.2.cloned.1.call-done = bf16[512,4096]{1,0:T(8,128)(2,1)} async-done(((bf16[512,128]{1,0:T(8,128)(2,1)}), bf16[512,4096]{1,0:T(8,128)(2,1)}) %all-gather.2.cloned.1.call-update) | async-done | bytes 4194320 | tf_op jit(solution)/shard_map/all_gather | solution.py:82
  335.3 4.1 fusion.129
  340.6 305.7 %all-reduce.3.cloned.1.call-done = f32[512,256]{1,0:T(8,128)} async-done(((f32[512,256]{1,0:T(8,128)}), f32[512,256]{1,0:T(8,128)}) %all-reduce.3.cloned.1.call-update) | async-done | bytes 524304 | tf_op jit(solution)/shard_map/psum | solution.py:87
  646.3 2.3 fusion.1
  648.6 92.5 %all-reduce.5.cloned.1.call-done = bf16[128,256]{1,0:T(8,128)(2,1)} async-done(((bf16[128,256]{1,0:T(8,128)(2,1)}), bf16[128,256]{1,0:T(8,128)(2,1)}) %all-reduce.5.cloned.1.call-update) | async-done | bytes 65552 | tf_op jit(solution)/shard_map/psum | solution.py:91
  741.1 1.5 convert_element_type.78
  742.6 1.9 copy.74
  (47 shorter events, 12.5 us)
Async XLA Ops:
  7.2 328.1 %copy-start = (bf16[4096,128]{1,0:T(8,128)(2,1)S(1)}, bf16[4096,128]{1,0:T(8,128)(2,1)}, u32[]{:S(2)}) copy-start(bf16[4096,128]{1,0:T(8,128)(2,1)} %param.10) | copy-start | bytes 3145732
  11.0 18.0 %all-to-all-start.1 = ((bf16[8,2,4096]{2,1,0:T(2,128)(2,1)}), bf16[8,2,4096]{2,1,0:T(2,128)(2,1)S(1)}, u32[]{:S(2)}, u32[]{:S(2)}) async-start(bf16[8,2,4096]{2,1,0:T(2,128)(2,1)} %reshape.151), calls=%async_computation.1 | async-start | bytes 262144 | tf_op jit(solution)/shard_map/all_to_all | solution.py:26
  29.0 12.9 %all-to-all-start = ((bf16[8,2,4096]{2,1,0:T(2,128)(2,1)}), bf16[8,2,4096]{2,1,0:T(2,128)(2,1)S(1)}, u32[]{:S(2)}, u32[]{:S(2)}) async-start(bf16[8,2,4096]{2,1,0:T(2,128)(2,1)} %reshape.153), calls=%async_computation | async-start | bytes 262144 | tf_op jit(solution)/shard_map/all_to_all | solution.py:25
  45.3 49.3 %all-to-all-start.2 = ((f32[4,16,64,128]{3,2,0,1:T(8,128)}), f32[4,16,64,128]{3,2,0,1:T(8,128)S(1)}, u32[]{:S(2)}, u32[]{:S(2)}) async-start(f32[4,16,64,128]{3,2,0,1:T(8,128)} %copy.41), calls=%async_computation.2 | async-start | bytes 4194304 | tf_op jit(solution)/shard_map/all_to_all | solution.py:43
  50.4 284.9 %all-gather.2.cloned.1.call-start = ((), (), s32[]{:S(2)}) async-start(), calls=%async_computation.5 | async-start | bytes 4325376 | tf_op jit(solution)/shard_map/all_gather | solution.py:82
  175.6 18.5 %copy-start.1 = (bf16[512,128]{1,0:T(8,128)(2,1)S(1)}, bf16[512,128]{1,0:T(8,128)(2,1)}, u32[]{:S(2)}) copy-start(bf16[512,128]{1,0:T(8,128)(2,1)} %param.6) | copy-start | bytes 393220
  175.6 18.4 %copy-start.2 = (bf16[512,128]{1,0:T(8,128)(2,1)S(1)}, bf16[512,128]{1,0:T(8,128)(2,1)}, u32[]{:S(2)}) copy-start(bf16[512,128]{1,0:T(8,128)(2,1)} %param.7) | copy-start | bytes 393220
  175.7 18.4 %copy-start.4 = (f32[128]{0:T(128)S(1)}, f32[128]{0:T(128)}, u32[]{:S(2)}) copy-start(f32[128]{0:T(128)} %param.9) | copy-start | bytes 1540
  194.8 144.5 %copy-start.3 = (bf16[128,256]{1,0:T(8,128)(2,1)S(1)}, bf16[128,256]{1,0:T(8,128)(2,1)}, u32[]{:S(2)}) copy-start(bf16[128,256]{1,0:T(8,128)(2,1)} %param.11) | copy-start | bytes 196612
  194.9 451.4 %all-reduce.3.cloned.1.call-start = ((), (), s32[]{:S(2)}) async-start(), calls=%async_computation.6 | async-start | bytes 1048576 | tf_op jit(solution)/shard_map/psum | solution.py:87
  340.6 400.6 %all-reduce.5.cloned.1.call-start = ((), (), s32[]{:S(2)}) async-start(), calls=%async_computation.7 | async-start | bytes 131072 | tf_op jit(solution)/shard_map/psum | solution.py:91
Sparse Core Ops, SparseCore 0:
  195.0 140.2 all-gather.1
  340.7 305.5 all-reduce.2
  649.7 91.4 all-reduce.4
where the time goes:
time: 752 us; the launch traced here: 751 us
  waiting for transfers between devices  594 us (79%)
  matrix products  53.9 us (7%)
  blocking collectives  52.5 us (7%)
  starting transfers between devices  20 us (3%)
  between operations  14 us (2%)
  local copies, waits for them, and re-layouts  10.4 us (1%)
    psum x1, waiting for transfers between devices, per_device(): sketch_y = lax.psum(partial_y, 'chan')  306 us
    all_gather x1, waiting for transfers between devices, per_device(): lax.all_gather(gated, 'chan', axis=1, tiled=True)  140 us
    psum x1, waiting for transfers between devices, per_device(): lax.psum(partial_z.astype(jnp.bfloat16), 'seq').astype(jnp.float32)  92.5 us
    all_to_all x1, waiting for transfers between devices, per_device(): lax.all_to_all(stacked, 'seq', split_axis=1, concat_axis=2, tiled=True)  44 us
    all_to_all x1, blocking collectives, per_device(): lax.all_to_all(jnp.stack([turned_re, turned_im]), 'seq', split_axis=2, co...  35.3 us
    all_to_all x1, blocking collectives, per_device(): lax.all_to_all(by_class / fft_len, 'seq', split_axis=0, concat_axis=1, ti...  17.1 us
  transfers between devices with their start and end apart: 6, of which 6 were waited for; matrix products, arithmetic and copies ran while one was open for 1% of the time, Pallas kernels for 0%

commit v1 on v0

v1 whole, which is shorter than its diff:
```python
import functools
import math

import jax
import jax.numpy as jnp
import numpy as np
from jax import lax
from jax.experimental import pallas as pl
from jax.experimental.pallas import tpu as pltpu
from jax.sharding import PartitionSpec as P

MESH = pl.DeviceIdType.MESH
F32, BF16 = jnp.float32, jnp.bfloat16

SEQ_DEV = 8
CHAN_DEV = 32
NEAR = 8
FAR = 4
ROWS = 512
CHANS = 128
SUB = 64
LANES = 16
COARSE = 9
RANK = 256


def split_np(x):
    high = x.astype(jnp.bfloat16)
    low = (x - high.astype(np.float64)).astype(jnp.bfloat16)
    return high, low


@functools.lru_cache(None)
def tables():
    n = 2 * SEQ_DEV * ROWS
    j = np.arange(SUB)
    q = np.arange(8)
    b = np.arange(8)
    turn = []
    fwd, inv = [], []
    eye = np.eye(LANES)
    for a in range(COARSE):
        k1 = a + 16 * b
        angle = 2 * np.pi * np.outer(j, k1) / n
        turn.append((np.repeat(np.cos(angle), LANES, 1), np.repeat(np.sin(angle), LANES, 1)))
        ang = 2 * np.pi * np.outer(q, k1) / 128
        c, s = np.kron(np.cos(ang), eye), np.kron(np.sin(ang), eye)
        fwd.append(np.block([[c, -s], [s, c]]))
        weight = (1.0 if a in (0, 8) else 2.0) / n
        inv.append(np.block([[c.T, s.T], [-s.T, c.T]]) * weight)
    fine = 2 * np.pi * np.outer(j, j) / SUB
    c, s = np.cos(fine), np.sin(fine)
    left = np.block([[c, s], [-s, c]])
    left_inv = np.block([[c, -s], [s, c]])

    def triple(m):
        high, low = split_np(m)
        return np.concatenate([high, high, low], 1)

    fwd_hi, fwd_lo = split_np(np.stack(fwd))
    inv_hi, inv_lo = split_np(np.stack(inv))
    turn = np.stack([np.stack(t) for t in turn]).astype(np.float32)
    return turn, np.stack([triple(left), triple(left_inv)]), fwd_hi, fwd_lo, inv_hi, inv_lo


def dot(a, b):
    return lax.dot_general(a, b, (((1,), (0,)), ((), ())), preferred_element_type=F32)


def split(x):
    high = x.astype(BF16)
    return high, (x - high.astype(F32)).astype(BF16)


def block_transpose(blocks):
    lane = lax.broadcasted_iota(jnp.int32, (SUB, 128), 1)
    for bit in range(3):
        step = LANES << bit
        low = (lane & step) == 0
        new = list(blocks)
        for q in range(8):
            if q >> bit & 1:
                continue
            p = q | 1 << bit
            new[q] = jnp.where(low, blocks[q], pltpu.roll(blocks[p], step, 1))
            new[p] = jnp.where(low, pltpu.roll(blocks[q], 128 - step, 1), blocks[p])
        blocks = new
    return blocks


def coarse_forward(x):
    plus = {s: x[s] + x[8 - s] for s in (1, 2, 3)}
    minus = {s: x[s] - x[8 - s] for s in (1, 2, 3)}

    def total(terms):
        out = None
        for factor, value in terms:
            if abs(factor) < 1e-9:
                continue
            if abs(factor - 1) < 1e-9:
                term = value
            elif abs(factor + 1) < 1e-9:
                term = -value
            else:
                term = value * np.float32(factor)
            out = term if out is None else out + term
        return jnp.zeros_like(x[0]) if out is None else out

    result = []
    for a in range(COARSE):
        cos = lambda s: math.cos(2 * math.pi * s * a / 16)
        sin = lambda s: math.sin(2 * math.pi * s * a / 16)
        even, odd = (plus, minus) if a % 2 == 0 else (minus, plus)
        re = total([(1.0, x[0]), (cos(4), x[4])] + [(cos(s), even[s]) for s in (1, 2, 3)])
        im = total([(-sin(4), x[4])] + [(-sin(s), odd[s]) for s in (1, 2, 3)])
        result.append((re, im))
    return result


def kernel(
    sig, gat, fil, skip, w, test, turn, left, fwd_hi, fwd_lo, inv_hi, inv_lo,
    mixed, out_y, out_z,
    send_a, recv_a, send_b, recv_b, depth, w_group, part, recv_p,
    send_y, recv_y, full_y, send_z, recv_z, full_z, spec, back,
    sem_a, sem_b, sem_g, sem_w, sem_p, sem_y, sem_v, sem_z, sem_t, sem_w0,
):
    me_s, me_c = lax.axis_index("seq"), lax.axis_index("chan")
    group, near = me_c // NEAR, me_c % NEAR

    def on_seq(k):
        return {"seq": lax.rem(me_s + k, SEQ_DEV), "chan": me_c}

    def on_chan(k):
        return {"seq": me_s, "chan": lax.rem(me_c + k, CHAN_DEV)}

    def on_near(k):
        return {"seq": me_s, "chan": group * NEAR + lax.rem(near + k, NEAR)}

    def on_far(k):
        return {"seq": me_s, "chan": lax.rem(me_c + NEAR * k, CHAN_DEV)}

    def remote(src, dst, sems, k, target):
        copy = pltpu.make_async_remote_copy(
            src_ref=src, dst_ref=dst, send_sem=sems.at[0, k], recv_sem=sems.at[1, k],
            device_id=target, device_id_type=MESH,
        )
        copy.start()
        return copy

    barrier = pltpu.get_barrier_semaphore()
    for k in range(1, SEQ_DEV):
        pl.semaphore_signal(barrier, inc=1, device_id=on_seq(k), device_id_type=MESH)
    for k in range(1, CHAN_DEV):
        pl.semaphore_signal(barrier, inc=1, device_id=on_chan(k), device_id_type=MESH)

    for at, source in enumerate((sig, fil)):
        blocks = [source[q * SUB : (q + 1) * SUB, :].astype(F32) for q in range(8)]
        for d, block in enumerate(block_transpose(blocks)):
            send_a[d, at * SUB : (at + 1) * SUB, :] = block.astype(BF16)

    pl.semaphore_wait(barrier, SEQ_DEV - 1 + CHAN_DEV - 1)

    copies_a = [
        remote(send_a.at[lax.rem(me_s + k, SEQ_DEV)], recv_a.at[me_s], sem_a, k, on_seq(k))
        for k in range(1, SEQ_DEV)
    ]
    recv_a[me_s] = send_a[me_s]
    columns = pl.ds(pl.multiple_of(group * CHANS, CHANS), CHANS)
    copies_w = []
    for k in range(1, FAR):
        target = lax.rem(group + k, FAR)
        rows = pl.ds(pl.multiple_of(target * NEAR * CHANS, NEAR * CHANS), NEAR * CHANS)
        copies_w.append(remote(w.at[rows, :], w_group.at[:, columns], sem_w, k, on_far(k)))
    own_rows = pl.ds(pl.multiple_of(group * NEAR * CHANS, NEAR * CHANS), NEAR * CHANS)
    own_w = pltpu.make_async_copy(w.at[own_rows, :], w_group.at[:, columns], sem_w0)
    own_w.start()
    for copy in copies_a:
        copy.wait()

    for at in range(2):
        blocks = [recv_a[s, at * SUB : (at + 1) * SUB, :].astype(F32) for s in range(SEQ_DEV)]
        for a, (re, im) in enumerate(coarse_forward(blocks)):
            spec[a, at * SUB : (at + 1) * SUB, :128] = re
            spec[a, at * SUB : (at + 1) * SUB, 128:] = im
    for a in range(COARSE):
        high, low = split(spec[a])
        z = dot(high, fwd_hi[a]) + dot(low, fwd_hi[a]) + dot(high, fwd_lo[a])
        cos, sin = turn[a, 0], turn[a, 1]
        halves = []
        for at in range(2):
            re, im = z[at * SUB : (at + 1) * SUB, :128], z[at * SUB : (at + 1) * SUB, 128:]
            halves.append(jnp.concatenate([re * cos + im * sin, im * cos - re * sin], 0))
        high, low = split(jnp.concatenate(halves, 1))
        f = dot(left[0], jnp.concatenate([high, low, high], 0))
        sr, si, fr, fi = f[:SUB, :128], f[SUB:, :128], f[:SUB, 128:], f[SUB:, 128:]
        high, low = split(jnp.concatenate([sr * fr - si * fi, sr * fi + si * fr], 0))
        g = dot(left[1], jnp.concatenate([high, low, high], 0))
        re, im = g[:SUB], g[SUB:]
        high, low = split(jnp.concatenate([re * cos - im * sin, im * cos + re * sin], 1))
        back[a] = dot(high, inv_hi[a]) + dot(low, inv_hi[a]) + dot(high, inv_lo[a])
    for s in range(5):
        sums = {}
        for a in range(COARSE):
            cos, sin = math.cos(2 * math.pi * s * a / 16), math.sin(2 * math.pi * s * a / 16)
            for name, factor, lanes in (("c", cos, 0), ("s", sin, 128)):
                if abs(factor) > 1e-9:
                    term = back[a, :, lanes : lanes + 128] * np.float32(factor)
                    key = name + "eo"[a % 2]
                    sums[key] = sums[key] + term if key in sums else term
        zero = jnp.zeros((SUB, 128), F32)
        ce, co, se, so = (sums.get(key, zero) for key in ("ce", "co", "se", "so"))
        send_b[s] = (ce + co - se - so).astype(BF16)
        if s in (1, 2, 3):
            send_b[8 - s] = (ce - co + se - so).astype(BF16)

    copies_b = [
        remote(send_b.at[lax.rem(me_s + k, SEQ_DEV)], recv_b.at[me_s], sem_b, k, on_seq(k))
        for k in range(1, SEQ_DEV)
    ]
    recv_b[me_s] = send_b[me_s]
    for copy in copies_b:
        copy.wait()
    near_columns = pl.ds(pl.multiple_of(near * CHANS, CHANS), CHANS)
    convolved = block_transpose([recv_b[d].astype(F32) for d in range(8)])
    for q in range(8):
        rows = slice(q * SUB, (q + 1) * SUB)
        value = convolved[q] + skip[...] * sig[rows, :].astype(F32)
        depth[rows, near_columns] = (gat[rows, :].astype(F32) * value).astype(BF16)

    copies_g = [
        remote(depth.at[:, near_columns], depth.at[:, near_columns], sem_g, k, on_near(k))
        for k in range(1, NEAR)
    ]
    own_w.wait()
    for copy in copies_w:
        copy.wait()
    for copy in copies_g:
        copy.wait()

    for f in range(FAR):
        lanes = slice(f * CHANS, (f + 1) * CHANS)
        part[f] = dot(depth[...], w_group[:, lanes]).astype(BF16)
    copies_p = [
        remote(part.at[lax.rem(group + k, FAR)], recv_p.at[group], sem_p, k, on_far(k))
        for k in range(1, FAR)
    ]
    recv_p[group] = part[group]
    for copy in copies_p:
        copy.wait()
    projected = recv_p[0].astype(F32)
    for f in range(1, FAR):
        projected = projected + recv_p[f].astype(F32)
    high, low = split(projected)
    mixed[...] = high
    partial_y = dot(high, test[...]) + dot(low, test[...])
    for c in range(CHAN_DEV):
        send_y[c] = partial_y[c * 16 : (c + 1) * 16, :].astype(BF16)
    copies_y = [
        remote(send_y.at[lax.rem(me_c + k, CHAN_DEV)], recv_y.at[me_c], sem_y, k, on_chan(k))
        for k in range(1, CHAN_DEV)
    ]
    recv_y[me_c] = send_y[me_c]
    for copy in copies_y:
        copy.wait()
    total = recv_y[0].astype(F32)
    for c in range(1, CHAN_DEV):
        total = total + recv_y[c].astype(F32)
    full_y[me_c] = total.astype(BF16)
    copies_v = [
        remote(full_y.at[me_c], full_y.at[me_c], sem_v, k, on_chan(k)) for k in range(1, CHAN_DEV)
    ]
    for copy in copies_v:
        copy.wait()
    sketch = full_y[...].reshape(ROWS, RANK)
    out_y[...] = sketch.astype(F32)
    partial_z = lax.dot_general(
        high, sketch, (((0,), (0,)), ((), ())), preferred_element_type=F32
    ) * np.float32(1.0 / (SEQ_DEV * ROWS))
    for s in range(SEQ_DEV):
        send_z[s] = partial_z[s * 16 : (s + 1) * 16, :].astype(BF16)
    copies_z = [
        remote(send_z.at[lax.rem(me_s + k, SEQ_DEV)], recv_z.at[me_s], sem_z, k, on_seq(k))
        for k in range(1, SEQ_DEV)
    ]
    recv_z[me_s] = send_z[me_s]
    for copy in copies_z:
        copy.wait()
    total = recv_z[0].astype(F32)
    for s in range(1, SEQ_DEV):
        total = total + recv_z[s].astype(F32)
    full_z[me_s] = total.astype(BF16)
    copies_t = [
        remote(full_z.at[me_s], full_z.at[me_s], sem_t, k, on_seq(k)) for k in range(1, SEQ_DEV)
    ]
    for copy in copies_t:
        copy.wait()
    out_z[...] = full_z[...].reshape(CHANS, RANK).astype(F32)


def per_device(signal, gating, filter_taps, skip_bias, out_weight, test_matrix):
    vmem = pl.BlockSpec(memory_space=pltpu.VMEM)
    constants = [jnp.asarray(t) for t in tables()]
    args = [signal, gating, filter_taps, skip_bias[None, :], out_weight, test_matrix] + constants

    def sems(n):
        return pltpu.SemaphoreType.DMA((2, n))

    return pl.pallas_call(
        kernel,
        out_shape=(
            jax.ShapeDtypeStruct((ROWS, CHANS), BF16),
            jax.ShapeDtypeStruct((ROWS, RANK), F32),
            jax.ShapeDtypeStruct((CHANS, RANK), F32),
        ),
        in_specs=[vmem] * len(args),
        out_specs=(vmem, vmem, vmem),
        scratch_shapes=[
            pltpu.VMEM((SEQ_DEV, 2 * SUB, 128), BF16),
            pltpu.VMEM((SEQ_DEV, 2 * SUB, 128), BF16),
            pltpu.VMEM((SEQ_DEV, SUB, 128), BF16),
            pltpu.VMEM((SEQ_DEV, SUB, 128), BF16),
            pltpu.VMEM((ROWS, NEAR * CHANS), BF16),
            pltpu.VMEM((NEAR * CHANS, FAR * CHANS), BF16),
            pltpu.VMEM((FAR, ROWS, CHANS), BF16),
            pltpu.VMEM((FAR, ROWS, CHANS), BF16),
            pltpu.VMEM((CHAN_DEV, 16, RANK), BF16),
            pltpu.VMEM((CHAN_DEV, 16, RANK), BF16),
            pltpu.VMEM((CHAN_DEV, 16, RANK), BF16),
            pltpu.VMEM((SEQ_DEV, 16, RANK), BF16),
            pltpu.VMEM((SEQ_DEV, 16, RANK), BF16),
            pltpu.VMEM((SEQ_DEV, 16, RANK), BF16),
            pltpu.VMEM((COARSE, 2 * SUB, 256), F32),
            pltpu.VMEM((COARSE, SUB, 256), F32),
            sems(SEQ_DEV), sems(SEQ_DEV), sems(NEAR), sems(FAR), sems(FAR),
            sems(CHAN_DEV), sems(CHAN_DEV), sems(SEQ_DEV), sems(SEQ_DEV),
            pltpu.SemaphoreType.DMA,
        ],
        compiler_params=pltpu.CompilerParams(
            collective_id=0, has_side_effects=True, vmem_limit_bytes=48 * 2**20
        ),
    )(*args)


def solution(mesh):
    return jax.shard_map(
        per_device,
        mesh=mesh,
        in_specs=(
            P("seq", "chan"), P("seq", "chan"), P("seq", "chan"),
            P("chan"), P(None, "chan"), P("chan", None),
        ),
        out_specs=(P("seq", "chan"), P("seq", None), P("chan", None)),
        check_vma=False,
    )
```

time: 752 us -> 92.8 us (0.12)
  waiting for transfers between devices: 594 us -> 0 us
  Pallas kernels: 0 us -> 79.6 us
  matrix products: 53.9 us -> 0 us
  blocking collectives: 52.5 us -> 0 us
  starting transfers between devices: 20 us -> 0 us
  between operations: 14 us -> 0.66 us
    psum x2 -> x0, waiting for transfers between devices: 398 us -> none  [the longest x1 306 us: per_device(): sketch_y = lax.psum(partial_y, 'chan')]
    all_gather x1 -> x0, waiting for transfers between devices: 140 us -> none  [per_device(): lax.all_gather(gated, 'chan', axis=1, tiled=True)]
    pallas_call x0 -> x1, Pallas kernels: none -> 79.6 us  [per_device(): pl.pallas_call(kernel, out_shape=(jax.ShapeDtypeStruct((ROWS, CHANS), BF1...]
    all_to_all x3 -> x0, waiting for transfers between devices: 55.6 us -> none  [the longest x1 44 us: per_device(): lax.all_to_all(stacked, 'seq', split_axis=1, concat_axis=2, tiled=True)]
    dot_general x15 -> x0, matrix products: 53.9 us -> none  [the longest x1 11 us: per_device(): sin_part = jnp.einsum('kb,sjbc->sjkc', big_sin, columns, precision=precise)]
    all_to_all x2 -> x0, blocking collectives: 52.5 us -> none  [the longest x1 35.3 us: per_device(): lax.all_to_all(jnp.stack([turned_re, turned_im]), 'seq', split_axis=2, co...]
    all_to_all x3 -> x0, starting transfers between devices: 19.9 us -> none  [the longest x1 9.97 us: per_device(): lax.all_to_all(filter_taps[None], 'seq', split_axis=1, concat_axis=0, til...]
    unnamed x18 -> x23, local copies, waits for them, and re-layouts: 4.08 us -> 12.1 us
  transfers between devices with their start and end apart: 6 -> 0, of which waited for: 6 -> 0; matrix products, arithmetic and copies ran while one was open for 1% -> 0% of each run, Pallas kernels for 0% -> 0%
where the time goes in v1:
time: 92.8 us; the launch traced here: 92.4 us
  Pallas kernels  79.6 us (86%)
  local copies, waits for them, and re-layouts  12.1 us (13%)
    pallas_call x1, Pallas kernels, per_device(): pl.pallas_call(kernel, out_shape=(jax.ShapeDtypeStruct((ROWS, CHANS), BF1...  79.6 us
    unnamed x23, local copies, waits for them, and re-layouts  12.1 us

profile of v1, /device:TPU:1, one launch (start us, length us, event | category | flops | bytes accessed | tf_op | source)
XLA Modules:
  0.0 92.4 jit_solution(7786745143342975969)
XLA Ops:
  0.6 0.0 copy-start
  0.6 1.3 %copy-done = bf16[9,256,256]{2,1,0:T(8,128)(2,1)S(1)} copy-done((bf16[9,256,256]{2,1,0:T(8,128)(2,1)S(1)}, bf16[9,256,256]{2,1,0:T(8,128)(2,1)}, u32[]{:S(2)}) %copy-start) | copy-done | bytes 1179672
  1.9 0.0 copy-start.1
  1.9 1.3 %copy-done.1 = bf16[9,256,256]{2,1,0:T(8,128)(2,1)S(1)} copy-done((bf16[9,256,256]{2,1,0:T(8,128)(2,1)S(1)}, bf16[9,256,256]{2,1,0:T(8,128)(2,1)}, u32[]{:S(2)}) %copy-start.1) | copy-done | bytes 1179672
  3.2 0.0 copy-start.2
  3.2 1.2 %copy-done.2 = bf16[4096,128]{1,0:T(8,128)(2,1)S(1)} copy-done((bf16[4096,128]{1,0:T(8,128)(2,1)S(1)}, bf16[4096,128]{1,0:T(8,128)(2,1)}, u32[]{:S(2)}) %copy-start.2) | copy-done | bytes 1048600
  4.4 0.0 copy-start.3
  4.4 1.1 %copy-done.3 = f32[9,2,64,128]{3,2,1,0:T(8,128)S(1)} copy-done((f32[9,2,64,128]{3,2,1,0:T(8,128)S(1)}, f32[9,2,64,128]{3,2,1,0:T(8,128)}, u32[]{:S(2)}) %copy-start.3) | copy-done | bytes 589848
  5.5 0.0 copy-start.4
  5.5 0.9 %copy-done.4 = bf16[2,128,384]{2,1,0:T(8,128)(2,1)S(1)} copy-done((bf16[2,128,384]{2,1,0:T(8,128)(2,1)S(1)}, bf16[2,128,384]{2,1,0:T(8,128)(2,1)}, u32[]{:S(2)}) %copy-start.4) | copy-done | bytes 196632
  6.4 0.0 copy-start.5
  6.4 0.9 copy-done.5
  7.3 0.0 copy-start.6
  7.3 0.9 copy-done.6
  8.2 0.0 copy-start.7
  8.2 0.9 copy-done.7
  9.1 0.0 copy-start.8
  9.1 0.8 copy-done.8
  9.9 0.0 copy-start.9
  10.0 0.7 copy-done.9
  10.6 79.6 %shard_map.139 = (bf16[512,128]{1,0:T(8,128)(2,1)S(1)}, f32[512,256]{1,0:T(8,128)S(1)}, f32[128,256]{1,0:T(8,128)S(1)}) custom-call(bf16[512,128]{1,0:T(8,128)(2,1)S(1)} %copy-done.5, bf16[512,128]{1,0:T(8,128)(2,1)S(1)} %copy-done.6, bf16[512,128]{1,0:T(8,128)(2,1)S(1)} %copy-done.7, f32[1,128]{1,0:T(1,128)S(1)} %bitcast.1, ...), custom_call_target="tpu_custom_call" | custom-call | tf_op jit(solution)/shard_map/pallas_call | solution.py:308
  90.3 0.7 copy.18
  90.9 0.8 copy.19
  91.7 0.7 copy.20
Async XLA Ops:
  0.6 1.3 %copy-start = (bf16[9,256,256]{2,1,0:T(8,128)(2,1)S(1)}, bf16[9,256,256]{2,1,0:T(8,128)(2,1)}, u32[]{:S(2)}) copy-start(bf16[9,256,256]{2,1,0:T(8,128)(2,1)} %constant.15.clone.fwd_lo) | copy-start | bytes 3538948
  1.9 1.3 %copy-start.1 = (bf16[9,256,256]{2,1,0:T(8,128)(2,1)S(1)}, bf16[9,256,256]{2,1,0:T(8,128)(2,1)}, u32[]{:S(2)}) copy-start(bf16[9,256,256]{2,1,0:T(8,128)(2,1)} %constant.14.clone.fwd_hi) | copy-start | bytes 3538948
  3.2 1.2 %copy-start.2 = (bf16[4096,128]{1,0:T(8,128)(2,1)S(1)}, bf16[4096,128]{1,0:T(8,128)(2,1)}, u32[]{:S(2)}) copy-start(bf16[4096,128]{1,0:T(8,128)(2,1)} %w.1) | copy-start | bytes 3145732
  4.4 1.1 %copy-start.3 = (f32[9,2,64,128]{3,2,1,0:T(8,128)S(1)}, f32[9,2,64,128]{3,2,1,0:T(8,128)}, u32[]{:S(2)}) copy-start(f32[9,2,64,128]{3,2,1,0:T(8,128)} %constant.12.clone.turn) | copy-start | bytes 1769476
  5.5 0.9 %copy-start.4 = (bf16[2,128,384]{2,1,0:T(8,128)(2,1)S(1)}, bf16[2,128,384]{2,1,0:T(8,128)(2,1)}, u32[]{:S(2)}) copy-start(bf16[2,128,384]{2,1,0:T(8,128)(2,1)} %constant.13.clone.left) | copy-start | bytes 589828
  6.4 0.9 copy-start.5
  7.3 0.9 copy-start.6
  8.2 0.9 copy-start.7
  9.1 0.8 copy-start.8
  9.9 0.7 copy-start.9

commit v2 on v1

v2 whole, which is shorter than its diff:
```python
import functools
import math

import jax
import jax.numpy as jnp
import numpy as np
from jax import lax
from jax.experimental import pallas as pl
from jax.experimental.pallas import tpu as pltpu
from jax.sharding import PartitionSpec as P

MESH = pl.DeviceIdType.MESH
F32, BF16 = jnp.float32, jnp.bfloat16

SEQ_DEV = 8
CHAN_DEV = 32
NEAR = 8
FAR = 4
ROWS = 512
CHANS = 128
SUB = 64
LANES = 16
COARSE = 9
RANK = 256
SLICE = RANK // NEAR
CHUNKS = 4
STEP = ROWS // CHUNKS
HALF = ROWS // 2
SEQ_ORDER = (4, 3, 5, 2, 6, 1, 7)


def split_np(x):
    high = x.astype(jnp.bfloat16)
    low = (x - high.astype(np.float64)).astype(jnp.bfloat16)
    return high, low


@functools.lru_cache(None)
def tables():
    n = 2 * SEQ_DEV * ROWS
    j = np.arange(SUB)
    q = np.arange(8)
    b = np.arange(8)
    turn = []
    fwd, inv = [], []
    eye = np.eye(LANES)
    for a in range(COARSE):
        k1 = a + 16 * b
        angle = 2 * np.pi * np.outer(j, k1) / n
        turn.append((np.repeat(np.cos(angle), LANES, 1), np.repeat(np.sin(angle), LANES, 1)))
        ang = 2 * np.pi * np.outer(q, k1) / 128
        c, s = np.kron(np.cos(ang), eye), np.kron(np.sin(ang), eye)
        fwd.append(np.block([[c, -s], [s, c]]))
        weight = (1.0 if a in (0, 8) else 2.0) / n
        inv.append(np.block([[c.T, s.T], [-s.T, c.T]]) * weight)
    fine = 2 * np.pi * np.outer(j, j) / SUB
    c, s = np.cos(fine), np.sin(fine)
    left = np.block([[c, s], [-s, c]])
    left_inv = np.block([[c, -s], [s, c]])

    def triple(m):
        high, low = split_np(m)
        return np.concatenate([high, high, low], 1)

    fwd = np.stack(split_np(np.stack(fwd)))
    inv = np.stack(split_np(np.stack(inv)))
    turn = np.stack([np.stack(t) for t in turn]).astype(np.float32)
    return turn, np.stack([triple(left), triple(left_inv)]), fwd, inv


def dot(a, b):
    return lax.dot_general(a, b, (((1,), (0,)), ((), ())), preferred_element_type=F32)


def split(x):
    high = x.astype(BF16)
    return high, (x - high.astype(F32)).astype(BF16)


def block_transpose(blocks):
    lane = lax.broadcasted_iota(jnp.int32, (SUB, 128), 1)
    for bit in range(3):
        step = LANES << bit
        low = (lane & step) == 0
        new = list(blocks)
        for q in range(8):
            if q >> bit & 1:
                continue
            p = q | 1 << bit
            new[q] = jnp.where(low, blocks[q], pltpu.roll(blocks[p], step, 1))
            new[p] = jnp.where(low, pltpu.roll(blocks[q], 128 - step, 1), blocks[p])
        blocks = new
    return blocks


def coarse_forward(x):
    plus = {s: x[s] + x[8 - s] for s in (1, 2, 3)}
    minus = {s: x[s] - x[8 - s] for s in (1, 2, 3)}

    def total(terms):
        out = None
        for factor, value in terms:
            if abs(factor) < 1e-9:
                continue
            if abs(factor - 1) < 1e-9:
                term = value
            elif abs(factor + 1) < 1e-9:
                term = -value
            else:
                term = value * np.float32(factor)
            out = term if out is None else out + term
        return jnp.zeros_like(x[0]) if out is None else out

    result = []
    for a in range(COARSE):
        cos = lambda s: math.cos(2 * math.pi * s * a / 16)
        sin = lambda s: math.sin(2 * math.pi * s * a / 16)
        even, odd = (plus, minus) if a % 2 == 0 else (minus, plus)
        re = total([(1.0, x[0]), (cos(4), x[4])] + [(cos(s), even[s]) for s in (1, 2, 3)])
        im = total([(-sin(4), x[4])] + [(-sin(s), odd[s]) for s in (1, 2, 3)])
        result.append((re, im))
    return result


def kernel(
    sig_in, gat_in, fil_in, skip_in, w, test_in, turn_in, left_in, fwd_in, inv_in,
    mixed, out_y, out_z,
    sig, gat, fil, skip, turn, left, fwd, inv, sem_in,
    send_a, recv_a, send_b, recv_b, depth, w_group, part, recv_p, spec, back,
    test, w_rows, send_v, recv_v, v_own, v_near, send_y, recv_y, full_y,
    part_z, send_z, recv_z, recv_h, full_z,
    sem_a, sem_b, sem_g, sem_w, sem_r, sem_e, sem_v, sem_u, sem_p, sem_q, sem_y, sem_c, sem_h, sem_f,
):
    me_s, me_c = lax.axis_index("seq"), lax.axis_index("chan")
    group, near, core = me_c // NEAR, me_c % NEAR, me_s % 2

    def on_seq(k):
        return {"seq": lax.rem(me_s + k, SEQ_DEV), "chan": me_c}

    def on_chan(k):
        return {"seq": me_s, "chan": lax.rem(me_c + k, CHAN_DEV)}

    def on_near(k):
        return {"seq": me_s, "chan": group * NEAR + lax.rem(near + k, NEAR)}

    def on_far(k):
        return {"seq": me_s, "chan": lax.rem(me_c + NEAR * k, CHAN_DEV)}

    other_core = {"seq": me_s + 1 - 2 * core, "chan": me_c}

    def remote(src, dst, sems, k, target):
        copy = pltpu.make_async_remote_copy(
            src_ref=src, dst_ref=dst, send_sem=sems.at[0, k], recv_sem=sems.at[1, k],
            device_id=target, device_id_type=MESH,
        )
        copy.start()
        return copy

    def local(k, src, dst):
        copy = pltpu.make_async_copy(src, dst, sem_in.at[k])
        copy.start()
        return copy

    def finish(*groups):
        for copies in groups:
            for copy in copies:
                copy.wait()

    in_sig = [local(0, sig_in, sig), local(1, fil_in, fil)]
    in_tables = [
        local(2, fwd_in, fwd), local(3, turn_in, turn), local(4, left_in, left), local(5, inv_in, inv)
    ]
    in_gate = [local(6, gat_in, gat), local(7, skip_in, skip)]

    barrier = pltpu.get_barrier_semaphore()
    for k in range(1, SEQ_DEV):
        pl.semaphore_signal(barrier, inc=1, device_id=on_seq(k), device_id_type=MESH)
    for k in range(1, CHAN_DEV):
        pl.semaphore_signal(barrier, inc=1, device_id=on_chan(k), device_id_type=MESH)

    finish(in_sig)
    for at, source in enumerate((sig, fil)):
        blocks = [source[q * SUB : (q + 1) * SUB, :].astype(F32) for q in range(8)]
        for d, block in enumerate(block_transpose(blocks)):
            send_a[d, at * SUB : (at + 1) * SUB, :] = block.astype(BF16)

    pl.semaphore_wait(barrier, SEQ_DEV - 1 + CHAN_DEV - 1)

    copies_a = [
        remote(send_a.at[lax.rem(me_s + k, SEQ_DEV)], recv_a.at[me_s], sem_a, k, on_seq(k))
        for k in SEQ_ORDER
    ]

    columns = pl.ds(pl.multiple_of(group * CHANS, CHANS), CHANS)
    copies_e, copies_r, copies_w = [], [], []

    def weight_rows(target, first, count):
        return pl.ds(pl.multiple_of(target * NEAR * CHANS + first, CHANS), count)

    for k in range(1, FAR):
        rows = weight_rows(lax.rem(group + k, FAR), me_s * CHANS, CHANS)
        copies_r.append(remote(w.at[rows, :], w_rows.at[:, columns], sem_r, k, on_far(k)))
        copies_e.append(remote(test_in, test.at[group], sem_e, k, on_far(k)))
    copies_r.append(local(8, w.at[weight_rows(group, me_s * CHANS, CHANS), :], w_rows.at[:, columns]))
    copies_e.append(local(9, test_in, test.at[group]))
    for k in range(1, FAR):
        rows = weight_rows(lax.rem(group + k, FAR), 0, NEAR * CHANS)
        copies_w.append(remote(w.at[rows, :], w_group.at[:, columns], sem_w, k, on_far(k)))
    copies_w.append(local(10, w.at[weight_rows(group, 0, NEAR * CHANS), :], w_group.at[:, columns]))
    recv_a[me_s] = send_a[me_s]

    finish(copies_r, copies_e)
    product = jnp.zeros((CHANS, RANK), F32)
    for f in range(FAR):
        product = product + dot(w_rows[:, f * CHANS : (f + 1) * CHANS], test[f])
    send_v[...] = product.T.reshape(NEAR, SLICE, CHANS)
    copies_v = [
        remote(send_v.at[lax.rem(near + k, NEAR)], recv_v.at[near], sem_v, k, on_near(k))
        for k in range(1, NEAR)
    ]
    recv_v[near] = send_v[near]

    finish(in_tables, copies_a)
    for at in range(2):
        blocks = [recv_a[s, at * SUB : (at + 1) * SUB, :].astype(F32) for s in range(SEQ_DEV)]
        for a, (re, im) in enumerate(coarse_forward(blocks)):
            spec[a, at * SUB : (at + 1) * SUB, :128] = re
            spec[a, at * SUB : (at + 1) * SUB, 128:] = im
    for a in range(COARSE):
        if a == COARSE // 2:
            finish(copies_v)
            total = recv_v[0]
            for n in range(1, NEAR):
                total = total + recv_v[n]
            v_own[...] = total.astype(BF16)
            v_lanes = pl.ds(pl.multiple_of(me_s * CHANS, CHANS), CHANS)
            copies_u = [
                remote(v_own, v_near.at[:, v_lanes], sem_u, k, on_seq(k)) for k in SEQ_ORDER
            ]
            v_near[:, v_lanes] = v_own[...]
        high, low = split(spec[a])
        z = dot(high, fwd[0, a]) + dot(low, fwd[0, a]) + dot(high, fwd[1, a])
        cos, sin = turn[a, 0], turn[a, 1]
        halves = []
        for at in range(2):
            re, im = z[at * SUB : (at + 1) * SUB, :128], z[at * SUB : (at + 1) * SUB, 128:]
            halves.append(jnp.concatenate([re * cos + im * sin, im * cos - re * sin], 0))
        high, low = split(jnp.concatenate(halves, 1))
        f = dot(left[0], jnp.concatenate([high, low, high], 0))
        sr, si, fr, fi = f[:SUB, :128], f[SUB:, :128], f[:SUB, 128:], f[SUB:, 128:]
        high, low = split(jnp.concatenate([sr * fr - si * fi, sr * fi + si * fr], 0))
        g = dot(left[1], jnp.concatenate([high, low, high], 0))
        re, im = g[:SUB], g[SUB:]
        high, low = split(jnp.concatenate([re * cos - im * sin, im * cos + re * sin], 1))
        back[a] = dot(high, inv[0, a]) + dot(low, inv[0, a]) + dot(high, inv[1, a])
    for s in range(5):
        sums = {}
        for a in range(COARSE):
            cos, sin = math.cos(2 * math.pi * s * a / 16), math.sin(2 * math.pi * s * a / 16)
            for name, factor, lanes in (("c", cos, 0), ("s", sin, 128)):
                if abs(factor) > 1e-9:
                    term = back[a, :, lanes : lanes + 128] * np.float32(factor)
                    key = name + "eo"[a % 2]
                    sums[key] = sums[key] + term if key in sums else term
        zero = jnp.zeros((SUB, 128), F32)
        ce, co, se, so = (sums.get(key, zero) for key in ("ce", "co", "se", "so"))
        send_b[s] = (ce + co - se - so).astype(BF16)
        if s in (1, 2, 3):
            send_b[8 - s] = (ce - co + se - so).astype(BF16)

    copies_b = [
        remote(send_b.at[lax.rem(me_s + k, SEQ_DEV)], recv_b.at[me_s], sem_b, k, on_seq(k))
        for k in SEQ_ORDER
    ]
    recv_b[me_s] = send_b[me_s]
    finish(in_gate, copies_b)
    near_columns = pl.ds(pl.multiple_of(near * CHANS, CHANS), CHANS)
    convolved = block_transpose([recv_b[d].astype(F32) for d in range(8)])
    copies_g = []
    for i in range(CHUNKS):
        for q in range(i * 8 // CHUNKS, (i + 1) * 8 // CHUNKS):
            rows = slice(q * SUB, (q + 1) * SUB)
            value = convolved[q] + skip[...] * sig[rows, :].astype(F32)
            depth[rows, near_columns] = (gat[rows, :].astype(F32) * value).astype(BF16)
        block = depth.at[i * STEP : (i + 1) * STEP, near_columns]
        copies_g.append([remote(block, block, sem_g, i * NEAR + k, on_near(k)) for k in range(1, NEAR)])

    copies_p, copies_q, copies_y = [], [], []
    y_block = near * FAR + group

    def sum_y(half):
        lanes = slice(half * HALF, (half + 1) * HALF)
        finish(copies_q[half])
        total = recv_y[0, :, lanes]
        for f in range(1, FAR):
            total = total + recv_y[f, :, lanes]
        full_y[y_block, :, lanes] = total
        block = full_y.at[y_block, :, lanes]
        copies_y.append(
            [remote(block, block, sem_y, half * CHAN_DEV + k, on_chan(k)) for k in range(1, CHAN_DEV)]
        )

    finish(copies_w, copies_u)
    for i in range(CHUNKS):
        rows = slice(i * STEP, (i + 1) * STEP)
        if i == CHUNKS - 1:
            sum_y(0)
        finish(copies_g[i])
        block = depth[rows, :]
        sketch = lax.dot_general(
            v_near[...], block, (((1,), (1,)), ((), ())), preferred_element_type=F32
        )
        for f in range(FAR):
            send_y[f, :, rows] = sketch[f * 8 : (f + 1) * 8, :]
        if i % (CHUNKS // 2) == CHUNKS // 2 - 1:
            half = i // (CHUNKS // 2)
            lanes = slice(half * HALF, (half + 1) * HALF)
            copies_q.append(
                [
                    remote(
                        send_y.at[lax.rem(group + k, FAR), :, lanes], recv_y.at[group, :, lanes],
                        sem_q, half * FAR + k, on_far(k),
                    )
                    for k in range(1, FAR)
                ]
            )
            recv_y[group, :, lanes] = send_y[group, :, lanes]
        projected = dot(block, w_group[...])
        for f in range(FAR):
            part[f, rows, :] = projected[:, f * CHANS : (f + 1) * CHANS].astype(BF16)
        copies_p.append(
            [
                remote(
                    part.at[lax.rem(group + k, FAR), rows, :], recv_p.at[group, rows, :],
                    sem_p, i * FAR + k, on_far(k),
                )
                for k in range(1, FAR)
            ]
        )
        recv_p[group, rows, :] = part[group, rows, :]
    sum_y(1)
    for i in range(CHUNKS):
        rows = slice(i * STEP, (i + 1) * STEP)
        finish(copies_p[i])
        total = recv_p[0, rows, :].astype(F32)
        for f in range(1, FAR):
            total = total + recv_p[f, rows, :].astype(F32)
        mixed[rows, :] = total.astype(BF16)

    sum_z = jnp.zeros((RANK, CHANS), F32)
    for half in range(2):
        lanes = slice(half * HALF, (half + 1) * HALF)
        finish(copies_y[half])
        sketch = full_y[:, :, lanes].reshape(RANK, HALF).astype(BF16)
        sum_z = sum_z + dot(sketch, mixed[lanes, :])
    part_z[...] = (sum_z * np.float32(1.0 / (SEQ_DEV * ROWS))).reshape(2, CHANS, CHANS)
    send_z[...] = part_z[1 - core].astype(BF16)
    copies_c = [remote(send_z, recv_z, sem_c, 0, other_core)]
    finish(copies_c)
    high = me_s // 2
    recv_h[high] = (part_z[core] + recv_z[...].astype(F32)).astype(BF16)
    copies_h = [remote(recv_h.at[high], recv_h.at[high], sem_h, k, on_seq(2 * k)) for k in (2, 1, 3)]
    out_y[...] = full_y[...].reshape(RANK, ROWS).T
    finish(copies_h)
    total = recv_h[0].astype(F32)
    for h in range(1, 4):
        total = total + recv_h[h].astype(F32)
    full_z[core] = total.astype(BF16)
    copies_f = [remote(full_z.at[core], full_z.at[core], sem_f, 0, other_core)]
    finish(copies_f)
    out_z[...] = full_z[...].reshape(RANK, CHANS).astype(F32).T


def store(*refs):
    ins, outs, held, sems = refs[:3], refs[3:6], refs[6:9], refs[9]
    first = [pltpu.make_async_copy(a, b, sems.at[0, k]) for k, (a, b) in enumerate(zip(ins, held))]
    second = [pltpu.make_async_copy(a, b, sems.at[1, k]) for k, (a, b) in enumerate(zip(held, outs))]
    for copy in first:
        copy.start()
    for k in range(3):
        first[k].wait()
        second[k].start()
    for copy in second:
        copy.wait()


def per_device(signal, gating, filter_taps, skip_bias, out_weight, test_matrix):
    vmem = pl.BlockSpec(memory_space=pltpu.VMEM)
    constants = [jnp.asarray(t) for t in tables()]
    args = [signal, gating, filter_taps, skip_bias[None, :], out_weight, test_matrix] + constants
    outs = (
        jax.ShapeDtypeStruct((ROWS, CHANS), BF16),
        jax.ShapeDtypeStruct((ROWS, RANK), F32),
        jax.ShapeDtypeStruct((CHANS, RANK), F32),
    )

    def sems(n):
        return pltpu.SemaphoreType.DMA((2, n))

    results = pl.pallas_call(
        kernel,
        out_shape=outs,
        in_specs=[pl.BlockSpec(memory_space=pl.ANY)] * len(args),
        out_specs=(vmem, vmem, vmem),
        scratch_shapes=[
            pltpu.VMEM((ROWS, CHANS), BF16),
            pltpu.VMEM((ROWS, CHANS), BF16),
            pltpu.VMEM((ROWS, CHANS), BF16),
            pltpu.VMEM((1, CHANS), F32),
        ]
        + [pltpu.VMEM(c.shape, c.dtype) for c in constants]
        + [
            pltpu.SemaphoreType.DMA((11,)),
            pltpu.VMEM((SEQ_DEV, 2 * SUB, 128), BF16),
            pltpu.VMEM((SEQ_DEV, 2 * SUB, 128), BF16),
            pltpu.VMEM((SEQ_DEV, SUB, 128), BF16),
            pltpu.VMEM((SEQ_DEV, SUB, 128), BF16),
            pltpu.VMEM((ROWS, NEAR * CHANS), BF16),
            pltpu.VMEM((NEAR * CHANS, FAR * CHANS), BF16),
            pltpu.VMEM((FAR, ROWS, CHANS), BF16),
            pltpu.VMEM((FAR, ROWS, CHANS), BF16),
            pltpu.VMEM((COARSE, 2 * SUB, 256), F32),
            pltpu.VMEM((COARSE, SUB, 256), F32),
            pltpu.VMEM((FAR, CHANS, RANK), BF16),
            pltpu.VMEM((CHANS, FAR * CHANS), BF16),
            pltpu.VMEM((NEAR, SLICE, CHANS), F32),
            pltpu.VMEM((NEAR, SLICE, CHANS), F32),
            pltpu.VMEM((SLICE, CHANS), BF16),
            pltpu.VMEM((SLICE, NEAR * CHANS), BF16),
            pltpu.VMEM((FAR, 8, ROWS), F32),
            pltpu.VMEM((FAR, 8, ROWS), F32),
            pltpu.VMEM((CHAN_DEV, 8, ROWS), F32),
            pltpu.VMEM((2, CHANS, CHANS), F32),
            pltpu.VMEM((CHANS, CHANS), BF16),
            pltpu.VMEM((CHANS, CHANS), BF16),
            pltpu.VMEM((4, CHANS, CHANS), BF16),
            pltpu.VMEM((2, CHANS, CHANS), BF16),
            sems(SEQ_DEV), sems(SEQ_DEV), sems(CHUNKS * NEAR), sems(FAR), sems(FAR), sems(FAR),
            sems(NEAR), sems(SEQ_DEV), sems(CHUNKS * FAR), sems(2 * FAR), sems(2 * CHAN_DEV),
            sems(1), sems(4), sems(1),
        ],
        compiler_params=pltpu.CompilerParams(
            collective_id=0, has_side_effects=True, vmem_limit_bytes=60 * 2**20
        ),
    )(*args)
    return pl.pallas_call(
        store,
        out_shape=outs,
        in_specs=[pl.BlockSpec(memory_space=pl.ANY)] * 3,
        out_specs=(pl.BlockSpec(memory_space=pl.ANY),) * 3,
        scratch_shapes=[pltpu.VMEM(o.shape, o.dtype) for o in outs]
        + [pltpu.SemaphoreType.DMA((2, 3))],
        compiler_params=pltpu.CompilerParams(vmem_limit_bytes=60 * 2**20),
    )(*results)


def solution(mesh):
    return jax.shard_map(
        per_device,
        mesh=mesh,
        in_specs=(
            P("seq", "chan"), P("seq", "chan"), P("seq", "chan"),
            P("chan"), P(None, "chan"), P("chan", None),
        ),
        out_specs=(P("seq", "chan"), P("seq", None), P("chan", None)),
        check_vma=False,
    )
```

time: 92.8 us -> 75.4 us (0.81)
  local copies, waits for them, and re-layouts: 12.1 us -> 0 us
  Pallas kernels: 79.6 us -> 74.7 us
    unnamed x23 -> x0, local copies, waits for them, and re-layouts: 12.1 us -> none
    pallas_call x1 -> x2, Pallas kernels: 79.6 us -> 74.7 us  [the longest x1 72.7 us: per_device(): pl.pallas_call(kernel, out_shape=outs, in_specs=[pl.BlockSpec(memory_spac...]
where the time goes in v2:
time: 75.4 us; the launch traced here: 75.3 us
  Pallas kernels  74.7 us (99%)
    pallas_call x1, Pallas kernels, per_device(): pl.pallas_call(kernel, out_shape=outs, in_specs=[pl.BlockSpec(memory_spac...  72.7 us
    pallas_call x1, Pallas kernels, per_device(): pl.pallas_call(store, out_shape=outs, in_specs=[pl.BlockSpec(memory_space...  2 us

profile of v2, /device:TPU:1, one launch (start us, length us, event | category | flops | bytes accessed | tf_op | source)
XLA Modules:
  0.0 75.3 jit_solution(4763195929535142234)
XLA Ops:
  0.6 72.7 %shard_map.121 = (bf16[512,128]{1,0:T(8,128)(2,1)}, f32[512,256]{1,0:T(8,128)}, f32[128,256]{1,0:T(8,128)}) custom-call(bf16[512,128]{1,0:T(8,128)(2,1)} %sig_in.1, bf16[512,128]{1,0:T(8,128)(2,1)} %gat_in.1, bf16[512,128]{1,0:T(8,128)(2,1)} %fil_in.1, f32[1,128]{1,0:T(1,128)} %bitcast.1, bf16[4096,128]{1,0:T(8,128)(2,1)} %w.1, bf16[128,256]{1,0:T(8,128)(2,1)} %test_in.1, ...), custom_call_target="tpu_custom_call" | custom-call | tf_op jit(solution)/shard_map/pallas_call | solution.py:400
  73.3 2.0 %shard_map.122 = (bf16[512,128]{1,0:T(8,128)(2,1)}, f32[512,256]{1,0:T(8,128)}, f32[128,256]{1,0:T(8,128)}) custom-call(bf16[512,128]{1,0:T(8,128)(2,1)} %get-tuple-element.6.refs_0_, f32[512,256]{1,0:T(8,128)} %get-tuple-element.7.refs_1_, f32[128,256]{1,0:T(8,128)} %get-tuple-element.8.refs_2_), custom_call_target="tpu_custom_call" | custom-call | tf_op jit(solution)/shard_map/pallas_call | solution.py:446

commit v3 on v2

--- a/solution.py
+++ b/solution.py
@@ -26,6 +26,7 @@
 CHUNKS = 4
 STEP = ROWS // CHUNKS
 HALF = ROWS // 2
+WEIGHT_HALF = NEAR * CHANS // 2
 SEQ_ORDER = (4, 3, 5, 2, 6, 1, 7)
 
 
@@ -127,9 +128,9 @@
     mixed, out_y, out_z,
     sig, gat, fil, skip, turn, left, fwd, inv, sem_in,
     send_a, recv_a, send_b, recv_b, depth, w_group, part, recv_p, spec, back,
-    test, w_rows, send_v, recv_v, v_own, v_near, send_y, recv_y, full_y,
+    test, w_rows, send_v, recv_v, v_own, v_near, send_y, recv_y, full_y, last_y,
     part_z, send_z, recv_z, recv_h, full_z,
-    sem_a, sem_b, sem_g, sem_w, sem_r, sem_e, sem_v, sem_u, sem_p, sem_q, sem_y, sem_c, sem_h, sem_f,
+    sem_a, sem_b, sem_g, sem_w, sem_r, sem_e, sem_v, sem_u, sem_p, sem_q, sem_y, sem_c, sem_h, sem_f, sem_k,
 ):
     me_s, me_c = lax.axis_index("seq"), lax.axis_index("chan")
     group, near, core = me_c // NEAR, me_c % NEAR, me_s % 2
@@ -203,41 +204,34 @@
         copies_e.append(remote(test_in, test.at[group], sem_e, k, on_far(k)))
     copies_r.append(local(8, w.at[weight_rows(group, me_s * CHANS, CHANS), :], w_rows.at[:, columns]))
     copies_e.append(local(9, test_in, test.at[group]))
+    half_rows = pl.ds(pl.multiple_of(core * WEIGHT_HALF, WEIGHT_HALF), WEIGHT_HALF)
+    w_half = w_group.at[half_rows, :]
     for k in range(1, FAR):
-        rows = weight_rows(lax.rem(group + k, FAR), 0, NEAR * CHANS)
-        copies_w.append(remote(w.at[rows, :], w_group.at[:, columns], sem_w, k, on_far(k)))
-    copies_w.append(local(10, w.at[weight_rows(group, 0, NEAR * CHANS), :], w_group.at[:, columns]))
+        rows = weight_rows(lax.rem(group + k, FAR), core * WEIGHT_HALF, WEIGHT_HALF)
+        copies_w.append(remote(w.at[rows, :], w_group.at[half_rows, columns], sem_w, k, on_far(k)))
+    rows = weight_rows(group, core * WEIGHT_HALF, WEIGHT_HALF)
+    copies_w.append(local(10, w.at[rows, :], w_group.at[half_rows, columns]))
     recv_a[me_s] = send_a[me_s]
 
     finish(copies_r, copies_e)
     product = jnp.zeros((CHANS, RANK), F32)
     for f in range(FAR):
         product = product + dot(w_rows[:, f * CHANS : (f + 1) * CHANS], test[f])
-    send_v[...] = product.T.reshape(NEAR, SLICE, CHANS)
+    send_v[...] = product.T.reshape(NEAR, SLICE, CHANS).astype(BF16)
+
+    finish(copies_a)
     copies_v = [
         remote(send_v.at[lax.rem(near + k, NEAR)], recv_v.at[near], sem_v, k, on_near(k))
         for k in range(1, NEAR)
     ]
     recv_v[near] = send_v[near]
-
-    finish(in_tables, copies_a)
+    finish(in_tables)
     for at in range(2):
         blocks = [recv_a[s, at * SUB : (at + 1) * SUB, :].astype(F32) for s in range(SEQ_DEV)]
         for a, (re, im) in enumerate(coarse_forward(blocks)):
             spec[a, at * SUB : (at + 1) * SUB, :128] = re
             spec[a, at * SUB : (at + 1) * SUB, 128:] = im
     for a in range(COARSE):
-        if a == COARSE // 2:
-            finish(copies_v)
-            total = recv_v[0]
-            for n in range(1, NEAR):
-                total = total + recv_v[n]
-            v_own[...] = total.astype(BF16)
-            v_lanes = pl.ds(pl.multiple_of(me_s * CHANS, CHANS), CHANS)
-            copies_u = [
-                remote(v_own, v_near.at[:, v_lanes], sem_u, k, on_seq(k)) for k in SEQ_ORDER
-            ]
-            v_near[:, v_lanes] = v_own[...]
         high, low = split(spec[a])
         z = dot(high, fwd[0, a]) + dot(low, fwd[0, a]) + dot(high, fwd[1, a])
         cos, sin = turn[a, 0], turn[a, 1]
@@ -273,6 +267,16 @@
         for k in SEQ_ORDER
     ]
     recv_b[me_s] = send_b[me_s]
+    finish(copies_v)
+    total = recv_v[0].astype(F32)
+    for n in range(1, NEAR):
+        total = total + recv_v[n].astype(F32)
+    v_own[...] = total.astype(BF16)
+    v_lanes = pl.ds(pl.multiple_of(me_s * CHANS, CHANS), CHANS)
+    copies_u = [remote(v_own, v_near.at[:, v_lanes], sem_u, k, on_seq(k)) for k in SEQ_ORDER]
+    v_near[:, v_lanes] = v_own[...]
+    finish(copies_w)
+    copies_k = [remote(w_half, w_half, sem_k, 0, other_core)]
     finish(in_gate, copies_b)
     near_columns = pl.ds(pl.multiple_of(near * CHANS, CHANS), CHANS)
     convolved = block_transpose([recv_b[d].astype(F32) for d in range(8)])
@@ -286,45 +290,41 @@
         copies_g.append([remote(block, block, sem_g, i * NEAR + k, on_near(k)) for k in range(1, NEAR)])
 
     copies_p, copies_q, copies_y = [], [], []
-    y_block = near * FAR + group
-
-    def sum_y(half):
-        lanes = slice(half * HALF, (half + 1) * HALF)
-        finish(copies_q[half])
-        total = recv_y[0, :, lanes]
+    y_rows = pl.ds(pl.multiple_of((near * FAR + group) * 8, 8), 8)
+
+    def sum_y():
+        finish(copies_q)
+        total = recv_y[0]
         for f in range(1, FAR):
-            total = total + recv_y[f, :, lanes]
-        full_y[y_block, :, lanes] = total
-        block = full_y.at[y_block, :, lanes]
-        copies_y.append(
-            [remote(block, block, sem_y, half * CHAN_DEV + k, on_chan(k)) for k in range(1, CHAN_DEV)]
-        )
-
-    finish(copies_w, copies_u)
+            total = total + recv_y[f]
+        full_y[y_rows, :HALF] = total
+        block = full_y.at[y_rows, :HALF]
+        copies_y.append([remote(block, block, sem_y, k, on_chan(k)) for k in range(1, CHAN_DEV)])
+
+    finish(copies_k, copies_u)
     for i in range(CHUNKS):
         rows = slice(i * STEP, (i + 1) * STEP)
         if i == CHUNKS - 1:
-            sum_y(0)
+            sum_y()
         finish(copies_g[i])
         block = depth[rows, :]
         sketch = lax.dot_general(
             v_near[...], block, (((1,), (1,)), ((), ())), preferred_element_type=F32
         )
-        for f in range(FAR):
-            send_y[f, :, rows] = sketch[f * 8 : (f + 1) * 8, :]
-        if i % (CHUNKS // 2) == CHUNKS // 2 - 1:
-            half = i // (CHUNKS // 2)
-            lanes = slice(half * HALF, (half + 1) * HALF)
-            copies_q.append(
-                [
-                    remote(
-                        send_y.at[lax.rem(group + k, FAR), :, lanes], recv_y.at[group, :, lanes],
-                        sem_q, half * FAR + k, on_far(k),
-                    )
-                    for k in range(1, FAR)
-                ]
-            )
-            recv_y[group, :, lanes] = send_y[group, :, lanes]
+        if i < CHUNKS // 2:
+            for f in range(FAR):
+                send_y[f, :, rows] = sketch[f * 8 : (f + 1) * 8, :]
+        else:
+            last_y[i % 2, me_c] = sketch.astype(BF16)
+            own = last_y.at[i % 2, me_c]
+            first = (i - 1) * CHAN_DEV
+            copies_y.append([remote(own, own, sem_y, first + k, on_chan(k)) for k in range(1, CHAN_DEV)])
+        if i == CHUNKS // 2 - 1:
+            copies_q = [
+                remote(send_y.at[lax.rem(group + k, FAR)], recv_y.at[group], sem_q, k, on_far(k))
+                for k in range(1, FAR)
+            ]
+            recv_y[group] = send_y[group]
         projected = dot(block, w_group[...])
         for f in range(FAR):
             part[f, rows, :] = projected[:, f * CHANS : (f + 1) * CHANS].astype(BF16)
@@ -338,7 +338,6 @@
             ]
         )
         recv_p[group, rows, :] = part[group, rows, :]
-    sum_y(1)
     for i in range(CHUNKS):
         rows = slice(i * STEP, (i + 1) * STEP)
         finish(copies_p[i])
@@ -347,12 +346,13 @@
             total = total + recv_p[f, rows, :].astype(F32)
         mixed[rows, :] = total.astype(BF16)
 
-    sum_z = jnp.zeros((RANK, CHANS), F32)
-    for half in range(2):
-        lanes = slice(half * HALF, (half + 1) * HALF)
-        finish(copies_y[half])
-        sketch = full_y[:, :, lanes].reshape(RANK, HALF).astype(BF16)
-        sum_z = sum_z + dot(sketch, mixed[lanes, :])
+    finish(*copies_y)
+    for i in range(CHUNKS // 2, CHUNKS):
+        total = last_y[i % 2, :NEAR].astype(F32)
+        for f in range(1, FAR):
+            total = total + last_y[i % 2, f * NEAR : (f + 1) * NEAR].astype(F32)
+        full_y[:, i * STEP : (i + 1) * STEP] = total.reshape(RANK, STEP)
+    sum_z = dot(full_y[...].astype(BF16), mixed[...])
     part_z[...] = (sum_z * np.float32(1.0 / (SEQ_DEV * ROWS))).reshape(2, CHANS, CHANS)
     send_z[...] = part_z[1 - core].astype(BF16)
     copies_c = [remote(send_z, recv_z, sem_c, 0, other_core)]
@@ -360,7 +360,7 @@
     high = me_s // 2
     recv_h[high] = (part_z[core] + recv_z[...].astype(F32)).astype(BF16)
     copies_h = [remote(recv_h.at[high], recv_h.at[high], sem_h, k, on_seq(2 * k)) for k in (2, 1, 3)]
-    out_y[...] = full_y[...].reshape(RANK, ROWS).T
+    out_y[...] = full_y[...].T
     finish(copies_h)
     total = recv_h[0].astype(F32)
     for h in range(1, 4):
@@ -423,21 +423,22 @@
             pltpu.VMEM((COARSE, SUB, 256), F32),
             pltpu.VMEM((FAR, CHANS, RANK), BF16),
             pltpu.VMEM((CHANS, FAR * CHANS), BF16),
-            pltpu.VMEM((NEAR, SLICE, CHANS), F32),
-            pltpu.VMEM((NEAR, SLICE, CHANS), F32),
+            pltpu.VMEM((NEAR, SLICE, CHANS), BF16),
+            pltpu.VMEM((NEAR, SLICE, CHANS), BF16),
             pltpu.VMEM((SLICE, CHANS), BF16),
             pltpu.VMEM((SLICE, NEAR * CHANS), BF16),
-            pltpu.VMEM((FAR, 8, ROWS), F32),
-            pltpu.VMEM((FAR, 8, ROWS), F32),
-            pltpu.VMEM((CHAN_DEV, 8, ROWS), F32),
+            pltpu.VMEM((FAR, 8, HALF), F32),
+            pltpu.VMEM((FAR, 8, HALF), F32),
+            pltpu.VMEM((RANK, ROWS), F32),
+            pltpu.VMEM((2, CHAN_DEV, SLICE, STEP), BF16),
             pltpu.VMEM((2, CHANS, CHANS), F32),
             pltpu.VMEM((CHANS, CHANS), BF16),
             pltpu.VMEM((CHANS, CHANS), BF16),
             pltpu.VMEM((4, CHANS, CHANS), BF16),
             pltpu.VMEM((2, CHANS, CHANS), BF16),
             sems(SEQ_DEV), sems(SEQ_DEV), sems(CHUNKS * NEAR), sems(FAR), sems(FAR), sems(FAR),
-            sems(NEAR), sems(SEQ_DEV), sems(CHUNKS * FAR), sems(2 * FAR), sems(2 * CHAN_DEV),
-            sems(1), sems(4), sems(1),
+            sems(NEAR), sems(SEQ_DEV), sems(CHUNKS * FAR), sems(FAR), sems(3 * CHAN_DEV),
+            sems(1), sems(4), sems(1), sems(1),
         ],
         compiler_params=pltpu.CompilerParams(
             collective_id=0, has_side_effects=True, vmem_limit_bytes=60 * 2**20

time: 75.4 us -> 72.5 us (0.962)
  Pallas kernels: 74.7 us -> 71.8 us
    pallas_call x1, Pallas kernels: 72.7 us -> 69.8 us  [per_device(): pl.pallas_call(kernel, out_shape=outs, in_specs=[pl.BlockSpec(memory_spac...]
where the time goes in v3:
time: 72.5 us; the launch traced here: 72.4 us
  Pallas kernels  71.8 us (99%)
    pallas_call x1, Pallas kernels, per_device(): pl.pallas_call(kernel, out_shape=outs, in_specs=[pl.BlockSpec(memory_spac...  69.8 us
    pallas_call x1, Pallas kernels, per_device(): pl.pallas_call(store, out_shape=outs, in_specs=[pl.BlockSpec(memory_space...  2 us

profile of v3, /device:TPU:1, one launch (start us, length us, event | category | flops | bytes accessed | tf_op | source)
XLA Modules:
  0.0 72.4 jit_solution(17112307990545851281)
XLA Ops:
  0.6 69.8 %shard_map.121 = (bf16[512,128]{1,0:T(8,128)(2,1)}, f32[512,256]{1,0:T(8,128)}, f32[128,256]{1,0:T(8,128)}) custom-call(bf16[512,128]{1,0:T(8,128)(2,1)} %sig_in.1, bf16[512,128]{1,0:T(8,128)(2,1)} %gat_in.1, bf16[512,128]{1,0:T(8,128)(2,1)} %fil_in.1, f32[1,128]{1,0:T(1,128)} %bitcast.1, bf16[4096,128]{1,0:T(8,128)(2,1)} %w.1, bf16[128,256]{1,0:T(8,128)(2,1)} %test_in.1, ...), custom_call_target="tpu_custom_call" | custom-call | tf_op jit(solution)/shard_map/pallas_call | solution.py:400
  70.4 2.0 %shard_map.122 = (bf16[512,128]{1,0:T(8,128)(2,1)}, f32[512,256]{1,0:T(8,128)}, f32[128,256]{1,0:T(8,128)}) custom-call(bf16[512,128]{1,0:T(8,128)(2,1)} %get-tuple-element.6.refs_0_, f32[512,256]{1,0:T(8,128)} %get-tuple-element.7.refs_1_, f32[128,256]{1,0:T(8,128)} %get-tuple-element.8.refs_2_), custom_call_target="tpu_custom_call" | custom-call | tf_op jit(solution)/shard_map/pallas_call | solution.py:447

commit v4 on v3

--- a/solution.py
+++ b/solution.py
@@ -25,7 +25,6 @@
 SLICE = RANK // NEAR
 CHUNKS = 4
 STEP = ROWS // CHUNKS
-HALF = ROWS // 2
 WEIGHT_HALF = NEAR * CHANS // 2
 SEQ_ORDER = (4, 3, 5, 2, 6, 1, 7)
 
@@ -128,7 +127,7 @@
     mixed, out_y, out_z,
     sig, gat, fil, skip, turn, left, fwd, inv, sem_in,
     send_a, recv_a, send_b, recv_b, depth, w_group, part, recv_p, spec, back,
-    test, w_rows, send_v, recv_v, v_own, v_near, send_y, recv_y, full_y, last_y,
+    test, w_rows, send_v, recv_v, v_own, v_near, part_y, near_y,
     part_z, send_z, recv_z, recv_h, full_z,
     sem_a, sem_b, sem_g, sem_w, sem_r, sem_e, sem_v, sem_u, sem_p, sem_q, sem_y, sem_c, sem_h, sem_f, sem_k,
 ):
@@ -137,9 +136,6 @@
 
     def on_seq(k):
         return {"seq": lax.rem(me_s + k, SEQ_DEV), "chan": me_c}
-
-    def on_chan(k):
-        return {"seq": me_s, "chan": lax.rem(me_c + k, CHAN_DEV)}
 
     def on_near(k):
         return {"seq": me_s, "chan": group * NEAR + lax.rem(near + k, NEAR)}
@@ -176,8 +172,10 @@
     barrier = pltpu.get_barrier_semaphore()
     for k in range(1, SEQ_DEV):
         pl.semaphore_signal(barrier, inc=1, device_id=on_seq(k), device_id_type=MESH)
-    for k in range(1, CHAN_DEV):
-        pl.semaphore_signal(barrier, inc=1, device_id=on_chan(k), device_id_type=MESH)
+    for k in range(1, NEAR):
+        pl.semaphore_signal(barrier, inc=1, device_id=on_near(k), device_id_type=MESH)
+    for k in range(1, FAR):
+        pl.semaphore_signal(barrier, inc=1, device_id=on_far(k), device_id_type=MESH)
 
     finish(in_sig)
     for at, source in enumerate((sig, fil)):
@@ -185,7 +183,7 @@
         for d, block in enumerate(block_transpose(blocks)):
             send_a[d, at * SUB : (at + 1) * SUB, :] = block.astype(BF16)
 
-    pl.semaphore_wait(barrier, SEQ_DEV - 1 + CHAN_DEV - 1)
+    pl.semaphore_wait(barrier, SEQ_DEV - 1 + NEAR - 1 + FAR - 1)
 
     copies_a = [
         remote(send_a.at[lax.rem(me_s + k, SEQ_DEV)], recv_a.at[me_s], sem_a, k, on_seq(k))
@@ -290,41 +288,26 @@
         copies_g.append([remote(block, block, sem_g, i * NEAR + k, on_near(k)) for k in range(1, NEAR)])
 
     copies_p, copies_q, copies_y = [], [], []
-    y_rows = pl.ds(pl.multiple_of((near * FAR + group) * 8, 8), 8)
-
-    def sum_y():
-        finish(copies_q)
-        total = recv_y[0]
+
+    def sum_y(i):
+        finish(copies_q[i])
+        total = part_y[i, 0]
         for f in range(1, FAR):
-            total = total + recv_y[f]
-        full_y[y_rows, :HALF] = total
-        block = full_y.at[y_rows, :HALF]
-        copies_y.append([remote(block, block, sem_y, k, on_chan(k)) for k in range(1, CHAN_DEV)])
+            total = total + part_y[i, f]
+        near_y[i, near] = total.astype(BF16)
+        own = near_y.at[i, near]
+        copies_y.append([remote(own, own, sem_y, i * NEAR + k, on_near(k)) for k in range(1, NEAR)])
 
     finish(copies_k, copies_u)
     for i in range(CHUNKS):
         rows = slice(i * STEP, (i + 1) * STEP)
-        if i == CHUNKS - 1:
-            sum_y()
         finish(copies_g[i])
         block = depth[rows, :]
-        sketch = lax.dot_general(
+        part_y[i, group] = lax.dot_general(
             v_near[...], block, (((1,), (1,)), ((), ())), preferred_element_type=F32
         )
-        if i < CHUNKS // 2:
-            for f in range(FAR):
-                send_y[f, :, rows] = sketch[f * 8 : (f + 1) * 8, :]
-        else:
-            last_y[i % 2, me_c] = sketch.astype(BF16)
-            own = last_y.at[i % 2, me_c]
-            first = (i - 1) * CHAN_DEV
-            copies_y.append([remote(own, own, sem_y, first + k, on_chan(k)) for k in range(1, CHAN_DEV)])
-        if i == CHUNKS // 2 - 1:
-            copies_q = [
-                remote(send_y.at[lax.rem(group + k, FAR)], recv_y.at[group], sem_q, k, on_far(k))
-                for k in range(1, FAR)
-            ]
-            recv_y[group] = send_y[group]
+        own = part_y.at[i, group]
+        copies_q.append([remote(own, own, sem_q, i * FAR + k, on_far(k)) for k in range(1, FAR)])
         projected = dot(block, w_group[...])
         for f in range(FAR):
             part[f, rows, :] = projected[:, f * CHANS : (f + 1) * CHANS].astype(BF16)
@@ -338,6 +321,9 @@
             ]
         )
         recv_p[group, rows, :] = part[group, rows, :]
+        if i:
+            sum_y(i - 1)
+    sum_y(CHUNKS - 1)
     for i in range(CHUNKS):
         rows = slice(i * STEP, (i + 1) * STEP)
         finish(copies_p[i])
@@ -346,13 +332,10 @@
             total = total + recv_p[f, rows, :].astype(F32)
         mixed[rows, :] = total.astype(BF16)
 
-    finish(*copies_y)
-    for i in range(CHUNKS // 2, CHUNKS):
-        total = last_y[i % 2, :NEAR].astype(F32)
-        for f in range(1, FAR):
-            total = total + last_y[i % 2, f * NEAR : (f + 1) * NEAR].astype(F32)
-        full_y[:, i * STEP : (i + 1) * STEP] = total.reshape(RANK, STEP)
-    sum_z = dot(full_y[...].astype(BF16), mixed[...])
+    sum_z = jnp.zeros((RANK, CHANS), F32)
+    for i in range(CHUNKS):
+        finish(copies_y[i])
+        sum_z = sum_z + dot(near_y[i].reshape(RANK, STEP), mixed[i * STEP : (i + 1) * STEP, :])
     part_z[...] = (sum_z * np.float32(1.0 / (SEQ_DEV * ROWS))).reshape(2, CHANS, CHANS)
     send_z[...] = part_z[1 - core].astype(BF16)
     copies_c = [remote(send_z, recv_z, sem_c, 0, other_core)]
@@ -360,7 +343,8 @@
     high = me_s // 2
     recv_h[high] = (part_z[core] + recv_z[...].astype(F32)).astype(BF16)
     copies_h = [remote(recv_h.at[high], recv_h.at[high], sem_h, k, on_seq(2 * k)) for k in (2, 1, 3)]
-    out_y[...] = full_y[...].T
+    for i in range(CHUNKS):
+        out_y[i * STEP : (i + 1) * STEP, :] = near_y[i].reshape(RANK, STEP).astype(F32).T
     finish(copies_h)
     total = recv_h[0].astype(F32)
     for h in range(1, 4):
@@ -427,17 +411,15 @@
             pltpu.VMEM((NEAR, SLICE, CHANS), BF16),
             pltpu.VMEM((SLICE, CHANS), BF16),
             pltpu.VMEM((SLICE, NEAR * CHANS), BF16),
-            pltpu.VMEM((FAR, 8, HALF), F32),
-            pltpu.VMEM((FAR, 8, HALF), F32),
-            pltpu.VMEM((RANK, ROWS), F32),
-            pltpu.VMEM((2, CHAN_DEV, SLICE, STEP), BF16),
+            pltpu.VMEM((CHUNKS, FAR, SLICE, STEP), F32),
+            pltpu.VMEM((CHUNKS, NEAR, SLICE, STEP), BF16),
             pltpu.VMEM((2, CHANS, CHANS), F32),
             pltpu.VMEM((CHANS, CHANS), BF16),
             pltpu.VMEM((CHANS, CHANS), BF16),
             pltpu.VMEM((4, CHANS, CHANS), BF16),
             pltpu.VMEM((2, CHANS, CHANS), BF16),
             sems(SEQ_DEV), sems(SEQ_DEV), sems(CHUNKS * NEAR), sems(FAR), sems(FAR), sems(FAR),
-            sems(NEAR), sems(SEQ_DEV), sems(CHUNKS * FAR), sems(FAR), sems(3 * CHAN_DEV),
+            sems(NEAR), sems(SEQ_DEV), sems(CHUNKS * FAR), sems(CHUNKS * FAR), sems(CHUNKS * NEAR),
             sems(1), sems(4), sems(1), sems(1),
         ],
         compiler_params=pltpu.CompilerParams(

time: 72.5 us -> 67.4 us (0.930)
  Pallas kernels: 71.8 us -> 66.6 us
    pallas_call x1, Pallas kernels: 69.8 us -> 64.6 us  [per_device(): pl.pallas_call(kernel, out_shape=outs, in_specs=[pl.BlockSpec(memory_spac...]
where the time goes in v4:
time: 67.4 us; the launch traced here: 67.3 us
  Pallas kernels  66.6 us (99%)
    pallas_call x1, Pallas kernels, per_device(): pl.pallas_call(kernel, out_shape=outs, in_specs=[pl.BlockSpec(memory_spac...  64.6 us
    pallas_call x1, Pallas kernels, per_device(): pl.pallas_call(store, out_shape=outs, in_specs=[pl.BlockSpec(memory_space...  2 us

profile of v4, /device:TPU:1, one launch (start us, length us, event | category | flops | bytes accessed | tf_op | source)
XLA Modules:
  0.0 67.3 jit_solution(15885831183407138936)
XLA Ops:
  0.6 64.6 %shard_map.121 = (bf16[512,128]{1,0:T(8,128)(2,1)}, f32[512,256]{1,0:T(8,128)}, f32[128,256]{1,0:T(8,128)}) custom-call(bf16[512,128]{1,0:T(8,128)(2,1)} %sig_in.1, bf16[512,128]{1,0:T(8,128)(2,1)} %gat_in.1, bf16[512,128]{1,0:T(8,128)(2,1)} %fil_in.1, f32[1,128]{1,0:T(1,128)} %bitcast.1, bf16[4096,128]{1,0:T(8,128)(2,1)} %w.1, bf16[128,256]{1,0:T(8,128)(2,1)} %test_in.1, ...), custom_call_target="tpu_custom_call" | custom-call | tf_op jit(solution)/shard_map/pallas_call | solution.py:384
  65.3 2.0 %shard_map.122 = (bf16[512,128]{1,0:T(8,128)(2,1)}, f32[512,256]{1,0:T(8,128)}, f32[128,256]{1,0:T(8,128)}) custom-call(bf16[512,128]{1,0:T(8,128)(2,1)} %get-tuple-element.6.refs_0_, f32[512,256]{1,0:T(8,128)} %get-tuple-element.7.refs_1_, f32[128,256]{1,0:T(8,128)} %get-tuple-element.8.refs_2_), custom_call_target="tpu_custom_call" | custom-call | tf_op jit(solution)/shard_map/pallas_call | solution.py:429

commit v5 on v4

--- a/solution.py
+++ b/solution.py
@@ -23,9 +23,9 @@
 COARSE = 9
 RANK = 256
 SLICE = RANK // NEAR
-CHUNKS = 4
+TOGETHER = 3
+CHUNKS = 2
 STEP = ROWS // CHUNKS
-WEIGHT_HALF = NEAR * CHANS // 2
 SEQ_ORDER = (4, 3, 5, 2, 6, 1, 7)
 
 
@@ -127,22 +127,34 @@
     mixed, out_y, out_z,
     sig, gat, fil, skip, turn, left, fwd, inv, sem_in,
     send_a, recv_a, send_b, recv_b, depth, w_group, part, recv_p, spec, back,
-    test, w_rows, send_v, recv_v, v_own, v_near, part_y, near_y,
+    test, w_rows, send_v, recv_v, v_near, part_y, near_y,
     part_z, send_z, recv_z, recv_h, full_z,
     sem_a, sem_b, sem_g, sem_w, sem_r, sem_e, sem_v, sem_u, sem_p, sem_q, sem_y, sem_c, sem_h, sem_f, sem_k,
 ):
     me_s, me_c = lax.axis_index("seq"), lax.axis_index("chan")
-    group, near, core = me_c // NEAR, me_c % NEAR, me_s % 2
+    core = me_s % 2
+    place = ((me_c // 2) % FAR, me_c // NEAR)
+    beside = me_c % 2
+    group = (place[1], place[0])
+    member = (2 * place[0] + beside, 2 * place[1] + beside)
 
     def on_seq(k):
         return {"seq": lax.rem(me_s + k, SEQ_DEV), "chan": me_c}
 
-    def on_near(k):
-        return {"seq": me_s, "chan": group * NEAR + lax.rem(near + k, NEAR)}
-
-    def on_far(k):
-        return {"seq": me_s, "chan": lax.rem(me_c + NEAR * k, CHAN_DEV)}
-
+    def on_line(o, k):
+        at = lax.rem(place[o] + k, FAR)
+        chan = NEAR * place[1] + 2 * at + beside if o == 0 else NEAR * at + 2 * place[0] + beside
+        return {"seq": me_s, "chan": chan}
+
+    def on_far(o, k):
+        return on_line(1 - o, k)
+
+    def on_member(o, k):
+        at = lax.rem(member[o] + k, NEAR)
+        chan = NEAR * place[1] + at if o == 0 else NEAR * (at // 2) + 2 * place[0] + at % 2
+        return {"seq": me_s, "chan": chan}
+
+    other_line = {"seq": me_s, "chan": me_c + 1 - 2 * beside}
     other_core = {"seq": me_s + 1 - 2 * core, "chan": me_c}
 
     def remote(src, dst, sems, k, target):
@@ -172,10 +184,9 @@
     barrier = pltpu.get_barrier_semaphore()
     for k in range(1, SEQ_DEV):
         pl.semaphore_signal(barrier, inc=1, device_id=on_seq(k), device_id_type=MESH)
-    for k in range(1, NEAR):
-        pl.semaphore_signal(barrier, inc=1, device_id=on_near(k), device_id_type=MESH)
-    for k in range(1, FAR):
-        pl.semaphore_signal(barrier, inc=1, device_id=on_far(k), device_id_type=MESH)
+    for o in range(2):
+        for k in range(1, NEAR):
+            pl.semaphore_signal(barrier, inc=1, device_id=on_member(o, k), device_id_type=MESH)
 
     finish(in_sig)
     for at, source in enumerate((sig, fil)):
@@ -183,68 +194,91 @@
         for d, block in enumerate(block_transpose(blocks)):
             send_a[d, at * SUB : (at + 1) * SUB, :] = block.astype(BF16)
 
-    pl.semaphore_wait(barrier, SEQ_DEV - 1 + NEAR - 1 + FAR - 1)
+    pl.semaphore_wait(barrier, SEQ_DEV - 1 + 2 * (NEAR - 1))
 
     copies_a = [
         remote(send_a.at[lax.rem(me_s + k, SEQ_DEV)], recv_a.at[me_s], sem_a, k, on_seq(k))
         for k in SEQ_ORDER
     ]
 
-    columns = pl.ds(pl.multiple_of(group * CHANS, CHANS), CHANS)
     copies_e, copies_r, copies_w = [], [], []
 
-    def weight_rows(target, first, count):
-        return pl.ds(pl.multiple_of(target * NEAR * CHANS + first, CHANS), count)
-
-    for k in range(1, FAR):
-        rows = weight_rows(lax.rem(group + k, FAR), me_s * CHANS, CHANS)
-        copies_r.append(remote(w.at[rows, :], w_rows.at[:, columns], sem_r, k, on_far(k)))
-        copies_e.append(remote(test_in, test.at[group], sem_e, k, on_far(k)))
-    copies_r.append(local(8, w.at[weight_rows(group, me_s * CHANS, CHANS), :], w_rows.at[:, columns]))
-    copies_e.append(local(9, test_in, test.at[group]))
-    half_rows = pl.ds(pl.multiple_of(core * WEIGHT_HALF, WEIGHT_HALF), WEIGHT_HALF)
-    w_half = w_group.at[half_rows, :]
-    for k in range(1, FAR):
-        rows = weight_rows(lax.rem(group + k, FAR), core * WEIGHT_HALF, WEIGHT_HALF)
-        copies_w.append(remote(w.at[rows, :], w_group.at[half_rows, columns], sem_w, k, on_far(k)))
-    rows = weight_rows(group, core * WEIGHT_HALF, WEIGHT_HALF)
-    copies_w.append(local(10, w.at[rows, :], w_group.at[half_rows, columns]))
+    def weight(o, target, part, count):
+        return w.at[target, pl.ds(part, count)] if o == 0 else w.at[pl.ds(part, count), target]
+
+    def weight_rows(o, target):
+        rows = pl.ds(pl.multiple_of(core * CHANS, CHANS), CHANS)
+        return w.at[target, me_s // 2, rows] if o == 0 else w.at[me_s // 2, target, rows]
+
+    columns = [pl.ds(pl.multiple_of(group[o] * CHANS, CHANS), CHANS) for o in range(2)]
+    for o in range(2):
+        for k in range(1, FAR):
+            rows = weight_rows(o, lax.rem(group[o] + k, FAR))
+            copies_r.append(
+                remote(rows, w_rows.at[o, :, columns[o]], sem_r, o * FAR + k, on_far(o, k))
+            )
+            copies_e.append(remote(test_in, test.at[o, group[o]], sem_e, o * FAR + k, on_far(o, k)))
+        copies_r.append(local(8 + o, weight_rows(o, group[o]), w_rows.at[o, :, columns[o]]))
+        copies_e.append(local(10 + o, test_in, test.at[o, group[o]]))
+    half = pl.ds(2 * core, 2)
+    for o in range(2):
+        target = w_group.at[o, half, :, columns[o]]
+        for k in range(1, FAR):
+            rows = weight(o, lax.rem(group[o] + k, FAR), 2 * core, 2)
+            copies_w.append(remote(rows, target, sem_w, o * FAR + k, on_far(o, k)))
+        copies_w.append(local(12 + o, weight(o, group[o], 2 * core, 2), target))
     recv_a[me_s] = send_a[me_s]
 
     finish(copies_r, copies_e)
-    product = jnp.zeros((CHANS, RANK), F32)
-    for f in range(FAR):
-        product = product + dot(w_rows[:, f * CHANS : (f + 1) * CHANS], test[f])
-    send_v[...] = product.T.reshape(NEAR, SLICE, CHANS).astype(BF16)
+    for o in range(2):
+        product = jnp.zeros((CHANS, RANK), F32)
+        for f in range(FAR):
+            product = product + dot(w_rows[o, :, f * CHANS : (f + 1) * CHANS], test[o, f])
+        send_v[o] = product.T.reshape(NEAR, SLICE, CHANS).astype(BF16)
 
     finish(copies_a)
-    copies_v = [
-        remote(send_v.at[lax.rem(near + k, NEAR)], recv_v.at[near], sem_v, k, on_near(k))
-        for k in range(1, NEAR)
-    ]
-    recv_v[near] = send_v[near]
+    copies_v = []
+    for o in range(2):
+        for k in range(1, NEAR):
+            block = send_v.at[o, lax.rem(member[o] + k, NEAR)]
+            copies_v.append(
+                remote(block, recv_v.at[o, member[o]], sem_v, o * NEAR + k, on_member(o, k))
+            )
+        recv_v[o, member[o]] = send_v[o, member[o]]
     finish(in_tables)
     for at in range(2):
         blocks = [recv_a[s, at * SUB : (at + 1) * SUB, :].astype(F32) for s in range(SEQ_DEV)]
         for a, (re, im) in enumerate(coarse_forward(blocks)):
             spec[a, at * SUB : (at + 1) * SUB, :128] = re
             spec[a, at * SUB : (at + 1) * SUB, 128:] = im
-    for a in range(COARSE):
-        high, low = split(spec[a])
-        z = dot(high, fwd[0, a]) + dot(low, fwd[0, a]) + dot(high, fwd[1, a])
-        cos, sin = turn[a, 0], turn[a, 1]
-        halves = []
-        for at in range(2):
-            re, im = z[at * SUB : (at + 1) * SUB, :128], z[at * SUB : (at + 1) * SUB, 128:]
-            halves.append(jnp.concatenate([re * cos + im * sin, im * cos - re * sin], 0))
-        high, low = split(jnp.concatenate(halves, 1))
-        f = dot(left[0], jnp.concatenate([high, low, high], 0))
-        sr, si, fr, fi = f[:SUB, :128], f[SUB:, :128], f[:SUB, 128:], f[SUB:, 128:]
-        high, low = split(jnp.concatenate([sr * fr - si * fi, sr * fi + si * fr], 0))
-        g = dot(left[1], jnp.concatenate([high, low, high], 0))
-        re, im = g[:SUB], g[SUB:]
-        high, low = split(jnp.concatenate([re * cos - im * sin, im * cos + re * sin], 1))
-        back[a] = dot(high, inv[0, a]) + dot(low, inv[0, a]) + dot(high, inv[1, a])
+    for first in range(0, COARSE, TOGETHER):
+        several = range(first, min(first + TOGETHER, COARSE))
+        pairs = [split(spec[a]) for a in several]
+        values = [
+            dot(high, fwd[0, a]) + dot(low, fwd[0, a]) + dot(high, fwd[1, a])
+            for a, (high, low) in zip(several, pairs)
+        ]
+        pairs = []
+        for a, z in zip(several, values):
+            cos, sin = turn[a, 0], turn[a, 1]
+            halves = []
+            for at in range(2):
+                re, im = z[at * SUB : (at + 1) * SUB, :128], z[at * SUB : (at + 1) * SUB, 128:]
+                halves.append(jnp.concatenate([re * cos + im * sin, im * cos - re * sin], 0))
+            pairs.append(split(jnp.concatenate(halves, 1)))
+        values = [dot(left[0], jnp.concatenate([high, low, high], 0)) for high, low in pairs]
+        pairs = []
+        for f in values:
+            sr, si, fr, fi = f[:SUB, :128], f[SUB:, :128], f[:SUB, 128:], f[SUB:, 128:]
+            pairs.append(split(jnp.concatenate([sr * fr - si * fi, sr * fi + si * fr], 0)))
+        values = [dot(left[1], jnp.concatenate([high, low, high], 0)) for high, low in pairs]
+        pairs = []
+        for a, g in zip(several, values):
+            cos, sin = turn[a, 0], turn[a, 1]
+            re, im = g[:SUB], g[SUB:]
+            pairs.append(split(jnp.concatenate([re * cos - im * sin, im * cos + re * sin], 1)))
+        for a, (high, low) in zip(several, pairs):
+            back[a] = dot(high, inv[0, a]) + dot(low, inv[0, a]) + dot(high, inv[1, a])
     for s in range(5):
         sums = {}
         for a in range(COARSE):
@@ -266,26 +300,39 @@
     ]
     recv_b[me_s] = send_b[me_s]
     finish(copies_v)
-    total = recv_v[0].astype(F32)
-    for n in range(1, NEAR):
-        total = total + recv_v[n].astype(F32)
-    v_own[...] = total.astype(BF16)
-    v_lanes = pl.ds(pl.multiple_of(me_s * CHANS, CHANS), CHANS)
-    copies_u = [remote(v_own, v_near.at[:, v_lanes], sem_u, k, on_seq(k)) for k in SEQ_ORDER]
-    v_near[:, v_lanes] = v_own[...]
+    for o in range(2):
+        total = recv_v[o, 0].astype(F32)
+        for n in range(1, NEAR):
+            total = total + recv_v[o, n].astype(F32)
+        v_near[me_s, o] = total.astype(BF16)
+    copies_u = [
+        remote(v_near.at[me_s], v_near.at[me_s], sem_u, k, on_seq(k)) for k in SEQ_ORDER
+    ]
     finish(copies_w)
-    copies_k = [remote(w_half, w_half, sem_k, 0, other_core)]
+    copies_k = [
+        remote(w_group.at[o, half], w_group.at[o, half], sem_k, o, other_core) for o in range(2)
+    ]
     finish(in_gate, copies_b)
-    near_columns = pl.ds(pl.multiple_of(near * CHANS, CHANS), CHANS)
+    own = [pl.ds(pl.multiple_of(member[o] * CHANS, CHANS), CHANS) for o in range(2)]
+    others = [
+        pl.ds(pl.multiple_of((member[o] + 1 - 2 * beside) * CHANS, CHANS), CHANS) for o in range(2)
+    ]
     convolved = block_transpose([recv_b[d].astype(F32) for d in range(8)])
-    copies_g = []
+    copies_g, copies_m = [], []
     for i in range(CHUNKS):
         for q in range(i * 8 // CHUNKS, (i + 1) * 8 // CHUNKS):
             rows = slice(q * SUB, (q + 1) * SUB)
             value = convolved[q] + skip[...] * sig[rows, :].astype(F32)
-            depth[rows, near_columns] = (gat[rows, :].astype(F32) * value).astype(BF16)
-        block = depth.at[i * STEP : (i + 1) * STEP, near_columns]
-        copies_g.append([remote(block, block, sem_g, i * NEAR + k, on_near(k)) for k in range(1, NEAR)])
+            depth[rows, own[i % 2]] = (gat[rows, :].astype(F32) * value).astype(BF16)
+        o, at = i % 2, i * NEAR
+        block = depth.at[i * STEP : (i + 1) * STEP, own[o]]
+        copies_m.append(remote(block, block, sem_g, at, other_line))
+        copies_g.append([remote(block, block, sem_g, at + k, on_line(o, k)) for k in range(1, FAR)])
+    for i in range(CHUNKS):
+        o, at = i % 2, i * NEAR + FAR
+        copies_m[i].wait()
+        block = depth.at[i * STEP : (i + 1) * STEP, others[o]]
+        copies_g[i] += [remote(block, block, sem_g, at + k, on_line(o, k)) for k in range(1, FAR)]
 
     copies_p, copies_q, copies_y = [], [], []
 
@@ -294,33 +341,37 @@
         total = part_y[i, 0]
         for f in range(1, FAR):
             total = total + part_y[i, f]
-        near_y[i, near] = total.astype(BF16)
-        own = near_y.at[i, near]
-        copies_y.append([remote(own, own, sem_y, i * NEAR + k, on_near(k)) for k in range(1, NEAR)])
+        o = i % 2
+        near_y[i, member[o]] = total.astype(BF16)
+        block = near_y.at[i, member[o]]
+        copies_y.append(
+            [remote(block, block, sem_y, i * NEAR + k, on_member(o, k)) for k in range(1, NEAR)]
+        )
 
     finish(copies_k, copies_u)
     for i in range(CHUNKS):
-        rows = slice(i * STEP, (i + 1) * STEP)
+        rows, o = slice(i * STEP, (i + 1) * STEP), i % 2
         finish(copies_g[i])
         block = depth[rows, :]
-        part_y[i, group] = lax.dot_general(
-            v_near[...], block, (((1,), (1,)), ((), ())), preferred_element_type=F32
+        product = jnp.concatenate([v_near[s, o] for s in range(SEQ_DEV)], 1)
+        part_y[i, group[o]] = lax.dot_general(
+            product, block, (((1,), (1,)), ((), ())), preferred_element_type=F32
         )
-        own = part_y.at[i, group]
-        copies_q.append([remote(own, own, sem_q, i * FAR + k, on_far(k)) for k in range(1, FAR)])
-        projected = dot(block, w_group[...])
+        sums = part_y.at[i, group[o]]
+        copies_q.append([remote(sums, sums, sem_q, i * FAR + k, on_far(o, k)) for k in range(1, FAR)])
+        projected = dot(block, w_group[o].reshape(NEAR * CHANS, FAR * CHANS))
         for f in range(FAR):
             part[f, rows, :] = projected[:, f * CHANS : (f + 1) * CHANS].astype(BF16)
         copies_p.append(
             [
                 remote(
-                    part.at[lax.rem(group + k, FAR), rows, :], recv_p.at[group, rows, :],
-                    sem_p, i * FAR + k, on_far(k),
+                    part.at[lax.rem(group[o] + k, FAR), rows, :], recv_p.at[group[o], rows, :],
+                    sem_p, i * FAR + k, on_far(o, k),
                 )
                 for k in range(1, FAR)
             ]
         )
-        recv_p[group, rows, :] = part[group, rows, :]
+        recv_p[group[o], rows, :] = part[group[o], rows, :]
         if i:
             sum_y(i - 1)
     sum_y(CHUNKS - 1)
@@ -371,7 +422,8 @@
 def per_device(signal, gating, filter_taps, skip_bias, out_weight, test_matrix):
     vmem = pl.BlockSpec(memory_space=pltpu.VMEM)
     constants = [jnp.asarray(t) for t in tables()]
-    args = [signal, gating, filter_taps, skip_bias[None, :], out_weight, test_matrix] + constants
+    weight = out_weight.reshape(FAR, FAR, 2 * CHANS, CHANS)
+    args = [signal, gating, filter_taps, skip_bias[None, :], weight, test_matrix] + constants
     outs = (
         jax.ShapeDtypeStruct((ROWS, CHANS), BF16),
         jax.ShapeDtypeStruct((ROWS, RANK), F32),
@@ -394,23 +446,22 @@
         ]
         + [pltpu.VMEM(c.shape, c.dtype) for c in constants]
         + [
-            pltpu.SemaphoreType.DMA((11,)),
+            pltpu.SemaphoreType.DMA((14,)),
             pltpu.VMEM((SEQ_DEV, 2 * SUB, 128), BF16),
             pltpu.VMEM((SEQ_DEV, 2 * SUB, 128), BF16),
             pltpu.VMEM((SEQ_DEV, SUB, 128), BF16),
             pltpu.VMEM((SEQ_DEV, SUB, 128), BF16),
             pltpu.VMEM((ROWS, NEAR * CHANS), BF16),
-            pltpu.VMEM((NEAR * CHANS, FAR * CHANS), BF16),
+            pltpu.VMEM((2, FAR, 2 * CHANS, FAR * CHANS), BF16),
             pltpu.VMEM((FAR, ROWS, CHANS), BF16),
             pltpu.VMEM((FAR, ROWS, CHANS), BF16),
             pltpu.VMEM((COARSE, 2 * SUB, 256), F32),
             pltpu.VMEM((COARSE, SUB, 256), F32),
-            pltpu.VMEM((FAR, CHANS, RANK), BF16),
-            pltpu.VMEM((CHANS, FAR * CHANS), BF16),
-            pltpu.VMEM((NEAR, SLICE, CHANS), BF16),
-            pltpu.VMEM((NEAR, SLICE, CHANS), BF16),
-            pltpu.VMEM((SLICE, CHANS), BF16),
-            pltpu.VMEM((SLICE, NEAR * CHANS), BF16),
+            pltpu.VMEM((2, FAR, CHANS, RANK), BF16),
+            pltpu.VMEM((2, CHANS, FAR * CHANS), BF16),
+            pltpu.VMEM((2, NEAR, SLICE, CHANS), BF16),
+            pltpu.VMEM((2, NEAR, SLICE, CHANS), BF16),
+            pltpu.VMEM((SEQ_DEV, 2, SLICE, CHANS), BF16),
             pltpu.VMEM((CHUNKS, FAR, SLICE, STEP), F32),
             pltpu.VMEM((CHUNKS, NEAR, SLICE, STEP), BF16),
             pltpu.VMEM((2, CHANS, CHANS), F32),
@@ -418,9 +469,9 @@
             pltpu.VMEM((CHANS, CHANS), BF16),
             pltpu.VMEM((4, CHANS, CHANS), BF16),
             pltpu.VMEM((2, CHANS, CHANS), BF16),
-            sems(SEQ_DEV), sems(SEQ_DEV), sems(CHUNKS * NEAR), sems(FAR), sems(FAR), sems(FAR),
-            sems(NEAR), sems(SEQ_DEV), sems(CHUNKS * FAR), sems(CHUNKS * FAR), sems(CHUNKS * NEAR),
-            sems(1), sems(4), sems(1), sems(1),
+            sems(SEQ_DEV), sems(SEQ_DEV), sems(CHUNKS * NEAR), sems(2 * FAR), sems(2 * FAR),
+            sems(2 * FAR), sems(2 * NEAR), sems(SEQ_DEV), sems(CHUNKS * FAR), sems(CHUNKS * FAR), sems(CHUNKS * NEAR),
+            sems(1), sems(4), sems(1), sems(2),
         ],
         compiler_params=pltpu.CompilerParams(
             collective_id=0, has_side_effects=True, vmem_limit_bytes=60 * 2**20

time: 67.4 us -> 61.4 us (0.911)
  Pallas kernels: 66.6 us -> 60.7 us
    pallas_call x1, Pallas kernels: 64.6 us -> 58.7 us  [per_device(): pl.pallas_call(kernel, out_shape=outs, in_specs=[pl.BlockSpec(memory_spac...]
where the time goes in v5:
time: 61.4 us; the launch traced here: 61.3 us
  Pallas kernels  60.7 us (99%)
  between operations  0.64 us (1%)
    pallas_call x1, Pallas kernels, per_device(): pl.pallas_call(kernel, out_shape=outs, in_specs=[pl.BlockSpec(memory_spac...  58.7 us
    pallas_call x1, Pallas kernels, per_device(): pl.pallas_call(store, out_shape=outs, in_specs=[pl.BlockSpec(memory_space...  2 us

profile of v5, /device:TPU:1, one launch (start us, length us, event | category | flops | bytes accessed | tf_op | source)
XLA Modules:
  0.0 61.3 jit_solution(9092865841042432468)
XLA Ops:
  0.6 58.7 %shard_map.121 = (bf16[512,128]{1,0:T(8,128)(2,1)}, f32[512,256]{1,0:T(8,128)}, f32[128,256]{1,0:T(8,128)}) custom-call(bf16[512,128]{1,0:T(8,128)(2,1)} %sig_in.1, bf16[512,128]{1,0:T(8,128)(2,1)} %gat_in.1, bf16[512,128]{1,0:T(8,128)(2,1)} %fil_in.1, f32[1,128]{1,0:T(1,128)} %bitcast.3, bf16[4,4,256,128]{3,2,1,0:T(8,128)(2,1)} %bitcast.2, ...), custom_call_target="tpu_custom_call" | custom-call | tf_op jit(solution)/shard_map/pallas_call | solution.py:436
  59.3 2.0 %shard_map.122 = (bf16[512,128]{1,0:T(8,128)(2,1)}, f32[512,256]{1,0:T(8,128)}, f32[128,256]{1,0:T(8,128)}) custom-call(bf16[512,128]{1,0:T(8,128)(2,1)} %get-tuple-element.6.refs_0_, f32[512,256]{1,0:T(8,128)} %get-tuple-element.7.refs_1_, f32[128,256]{1,0:T(8,128)} %get-tuple-element.8.refs_2_), custom_call_target="tpu_custom_call" | custom-call | tf_op jit(solution)/shard_map/pallas_call | solution.py:480

commit v6 on v5

--- a/solution.py
+++ b/solution.py
@@ -124,6 +124,7 @@
 
 def kernel(
     sig_in, gat_in, fil_in, skip_in, w, test_in, turn_in, left_in, fwd_in, inv_in,
+    to_mixed, to_y, to_z,
     mixed, out_y, out_z,
     sig, gat, fil, skip, turn, left, fwd, inv, sem_in,
     send_a, recv_a, send_b, recv_b, depth, w_group, part, recv_p, spec, back,
@@ -157,12 +158,15 @@
     other_line = {"seq": me_s, "chan": me_c + 1 - 2 * beside}
     other_core = {"seq": me_s + 1 - 2 * core, "chan": me_c}
 
+    sending = []
+
     def remote(src, dst, sems, k, target):
         copy = pltpu.make_async_remote_copy(
             src_ref=src, dst_ref=dst, send_sem=sems.at[0, k], recv_sem=sems.at[1, k],
             device_id=target, device_id_type=MESH,
         )
         copy.start()
+        sending.append(copy)
         return copy
 
     def local(k, src, dst):
@@ -173,7 +177,15 @@
     def finish(*groups):
         for copies in groups:
             for copy in copies:
-                copy.wait()
+                if copy.is_remote:
+                    copy.wait_recv()
+                else:
+                    copy.wait()
+
+    def settle():
+        for copy in sending:
+            copy.wait_send()
+        sending.clear()
 
     in_sig = [local(0, sig_in, sig), local(1, fil_in, fil)]
     in_tables = [
@@ -330,7 +342,7 @@
         copies_g.append([remote(block, block, sem_g, at + k, on_line(o, k)) for k in range(1, FAR)])
     for i in range(CHUNKS):
         o, at = i % 2, i * NEAR + FAR
-        copies_m[i].wait()
+        copies_m[i].wait_recv()
         block = depth.at[i * STEP : (i + 1) * STEP, others[o]]
         copies_g[i] += [remote(block, block, sem_g, at + k, on_line(o, k)) for k in range(1, FAR)]
 
@@ -359,7 +371,9 @@
         )
         sums = part_y.at[i, group[o]]
         copies_q.append([remote(sums, sums, sem_q, i * FAR + k, on_far(o, k)) for k in range(1, FAR)])
-        projected = dot(block, w_group[o].reshape(NEAR * CHANS, FAR * CHANS))
+    for i in range(CHUNKS):
+        rows, o = slice(i * STEP, (i + 1) * STEP), i % 2
+        projected = dot(depth[rows, :], w_group[o].reshape(NEAR * CHANS, FAR * CHANS))
         for f in range(FAR):
             part[f, rows, :] = projected[:, f * CHANS : (f + 1) * CHANS].astype(BF16)
         copies_p.append(
@@ -372,9 +386,8 @@
             ]
         )
         recv_p[group[o], rows, :] = part[group[o], rows, :]
-        if i:
-            sum_y(i - 1)
-    sum_y(CHUNKS - 1)
+    for i in range(CHUNKS):
+        sum_y(i)
     for i in range(CHUNKS):
         rows = slice(i * STEP, (i + 1) * STEP)
         finish(copies_p[i])
@@ -382,6 +395,7 @@
         for f in range(1, FAR):
             total = total + recv_p[f, rows, :].astype(F32)
         mixed[rows, :] = total.astype(BF16)
+    stores = [local(14, mixed, to_mixed)]
 
     sum_z = jnp.zeros((RANK, CHANS), F32)
     for i in range(CHUNKS):
@@ -396,6 +410,8 @@
     copies_h = [remote(recv_h.at[high], recv_h.at[high], sem_h, k, on_seq(2 * k)) for k in (2, 1, 3)]
     for i in range(CHUNKS):
         out_y[i * STEP : (i + 1) * STEP, :] = near_y[i].reshape(RANK, STEP).astype(F32).T
+    stores.append(local(15, out_y, to_y))
+    settle()
     finish(copies_h)
     total = recv_h[0].astype(F32)
     for h in range(1, 4):
@@ -404,6 +420,9 @@
     copies_f = [remote(full_z.at[core], full_z.at[core], sem_f, 0, other_core)]
     finish(copies_f)
     out_z[...] = full_z[...].reshape(RANK, CHANS).astype(F32).T
+    stores.append(local(16, out_z, to_z))
+    settle()
+    finish(stores)
 
 
 def store(*refs):
@@ -420,7 +439,6 @@
 
 
 def per_device(signal, gating, filter_taps, skip_bias, out_weight, test_matrix):
-    vmem = pl.BlockSpec(memory_space=pltpu.VMEM)
     constants = [jnp.asarray(t) for t in tables()]
     weight = out_weight.reshape(FAR, FAR, 2 * CHANS, CHANS)
     args = [signal, gating, filter_taps, skip_bias[None, :], weight, test_matrix] + constants
@@ -437,8 +455,9 @@
         kernel,
         out_shape=outs,
         in_specs=[pl.BlockSpec(memory_space=pl.ANY)] * len(args),
-        out_specs=(vmem, vmem, vmem),
-        scratch_shapes=[
+        out_specs=(pl.BlockSpec(memory_space=pl.ANY),) * 3,
+        scratch_shapes=[pltpu.VMEM(o.shape, o.dtype) for o in outs]
+        + [
             pltpu.VMEM((ROWS, CHANS), BF16),
             pltpu.VMEM((ROWS, CHANS), BF16),
             pltpu.VMEM((ROWS, CHANS), BF16),
@@ -446,7 +465,7 @@
         ]
         + [pltpu.VMEM(c.shape, c.dtype) for c in constants]
         + [
-            pltpu.SemaphoreType.DMA((14,)),
+            pltpu.SemaphoreType.DMA((17,)),
             pltpu.VMEM((SEQ_DEV, 2 * SUB, 128), BF16),
             pltpu.VMEM((SEQ_DEV, 2 * SUB, 128), BF16),
             pltpu.VMEM((SEQ_DEV, SUB, 128), BF16),

time: 61.4 us -> 59.9 us (0.976)
  Pallas kernels: 60.7 us -> 59.1 us
    pallas_call x1, Pallas kernels: 58.7 us -> 57.1 us  [per_device(): pl.pallas_call(kernel, out_shape=outs, in_specs=[pl.BlockSpec(memory_spac...]
where the time goes in v6:
time: 59.9 us; the launch traced here: 59.8 us
  Pallas kernels  59.1 us (99%)
  between operations  0.64 us (1%)
    pallas_call x1, Pallas kernels, per_device(): pl.pallas_call(kernel, out_shape=outs, in_specs=[pl.BlockSpec(memory_spac...  57.1 us
    pallas_call x1, Pallas kernels, per_device(): pl.pallas_call(store, out_shape=outs, in_specs=[pl.BlockSpec(memory_space...  2 us

profile of v6, /device:TPU:1, one launch (start us, length us, event | category | flops | bytes accessed | tf_op | source)
XLA Modules:
  0.0 59.8 jit_solution(10324428140484480922)
XLA Ops:
  0.6 57.1 %shard_map.121 = (bf16[512,128]{1,0:T(8,128)(2,1)}, f32[512,256]{1,0:T(8,128)}, f32[128,256]{1,0:T(8,128)}) custom-call(bf16[512,128]{1,0:T(8,128)(2,1)} %sig_in.1, bf16[512,128]{1,0:T(8,128)(2,1)} %gat_in.1, bf16[512,128]{1,0:T(8,128)(2,1)} %fil_in.1, f32[1,128]{1,0:T(1,128)} %bitcast.3, bf16[4,4,256,128]{3,2,1,0:T(8,128)(2,1)} %bitcast.2, ...), custom_call_target="tpu_custom_call" | custom-call | tf_op jit(solution)/shard_map/pallas_call | solution.py:454
  57.8 2.0 %shard_map.122 = (bf16[512,128]{1,0:T(8,128)(2,1)}, f32[512,256]{1,0:T(8,128)}, f32[128,256]{1,0:T(8,128)}) custom-call(bf16[512,128]{1,0:T(8,128)(2,1)} %get-tuple-element.6.refs_0_, f32[512,256]{1,0:T(8,128)} %get-tuple-element.7.refs_1_, f32[128,256]{1,0:T(8,128)} %get-tuple-element.8.refs_2_), custom_call_target="tpu_custom_call" | custom-call | tf_op jit(solution)/shard_map/pallas_call | solution.py:499

commit v7 on v6

--- a/solution.py
+++ b/solution.py
@@ -24,7 +24,7 @@
 RANK = 256
 SLICE = RANK // NEAR
 TOGETHER = 3
-CHUNKS = 2
+CHUNKS = 4
 STEP = ROWS // CHUNKS
 SEQ_ORDER = (4, 3, 5, 2, 6, 1, 7)
 
@@ -350,9 +350,9 @@
 
     def sum_y(i):
         finish(copies_q[i])
-        total = part_y[i, 0]
+        total = part_y[i, 0].astype(F32)
         for f in range(1, FAR):
-            total = total + part_y[i, f]
+            total = total + part_y[i, f].astype(F32)
         o = i % 2
         near_y[i, member[o]] = total.astype(BF16)
         block = near_y.at[i, member[o]]
@@ -368,7 +368,7 @@
         product = jnp.concatenate([v_near[s, o] for s in range(SEQ_DEV)], 1)
         part_y[i, group[o]] = lax.dot_general(
             product, block, (((1,), (1,)), ((), ())), preferred_element_type=F32
-        )
+        ).astype(BF16)
         sums = part_y.at[i, group[o]]
         copies_q.append([remote(sums, sums, sem_q, i * FAR + k, on_far(o, k)) for k in range(1, FAR)])
     for i in range(CHUNKS):
@@ -481,7 +481,7 @@
             pltpu.VMEM((2, NEAR, SLICE, CHANS), BF16),
             pltpu.VMEM((2, NEAR, SLICE, CHANS), BF16),
             pltpu.VMEM((SEQ_DEV, 2, SLICE, CHANS), BF16),
-            pltpu.VMEM((CHUNKS, FAR, SLICE, STEP), F32),
+            pltpu.VMEM((CHUNKS, FAR, SLICE, STEP), BF16),
             pltpu.VMEM((CHUNKS, NEAR, SLICE, STEP), BF16),
             pltpu.VMEM((2, CHANS, CHANS), F32),
             pltpu.VMEM((CHANS, CHANS), BF16),

time: 59.9 us -> 58.2 us (0.972)
  Pallas kernels: 59.1 us -> 57.4 us
    pallas_call x1, Pallas kernels: 57.1 us -> 55.4 us  [per_device(): pl.pallas_call(kernel, out_shape=outs, in_specs=[pl.BlockSpec(memory_spac...]
where the time goes in v7:
time: 58.2 us; the launch traced here: 58.1 us
  Pallas kernels  57.4 us (99%)
  between operations  0.64 us (1%)
    pallas_call x1, Pallas kernels, per_device(): pl.pallas_call(kernel, out_shape=outs, in_specs=[pl.BlockSpec(memory_spac...  55.4 us
    pallas_call x1, Pallas kernels, per_device(): pl.pallas_call(store, out_shape=outs, in_specs=[pl.BlockSpec(memory_space...  2 us

profile of v7, /device:TPU:1, one launch (start us, length us, event | category | flops | bytes accessed | tf_op | source)
XLA Modules:
  0.0 58.1 jit_solution(5892820421544934526)
XLA Ops:
  0.6 55.4 %shard_map.121 = (bf16[512,128]{1,0:T(8,128)(2,1)}, f32[512,256]{1,0:T(8,128)}, f32[128,256]{1,0:T(8,128)}) custom-call(bf16[512,128]{1,0:T(8,128)(2,1)} %sig_in.1, bf16[512,128]{1,0:T(8,128)(2,1)} %gat_in.1, bf16[512,128]{1,0:T(8,128)(2,1)} %fil_in.1, f32[1,128]{1,0:T(1,128)} %bitcast.3, bf16[4,4,256,128]{3,2,1,0:T(8,128)(2,1)} %bitcast.2, ...), custom_call_target="tpu_custom_call" | custom-call | tf_op jit(solution)/shard_map/pallas_call | solution.py:454
  56.1 2.0 %shard_map.122 = (bf16[512,128]{1,0:T(8,128)(2,1)}, f32[512,256]{1,0:T(8,128)}, f32[128,256]{1,0:T(8,128)}) custom-call(bf16[512,128]{1,0:T(8,128)(2,1)} %get-tuple-element.6.refs_0_, f32[512,256]{1,0:T(8,128)} %get-tuple-element.7.refs_1_, f32[128,256]{1,0:T(8,128)} %get-tuple-element.8.refs_2_), custom_call_target="tpu_custom_call" | custom-call | tf_op jit(solution)/shard_map/pallas_call | solution.py:499
